TPU v7x, 256 devices: a whole 4x4x8 slice. The times are simulated.
256 devices in a mesh: res: 256 (over x, y, z, core).
Axes of the slice: x: 4, y: 4, z: 8, core: 2. Of those that a mesh axis runs over, the one named last changes fastest.
Arguments:
- homolog_features: bfloat16 [256, 6144, 256], P(None, 'res'), may hold values from -6 to 6
- standardize_scale: float32 [256], replicated, may hold values from 0.25 to 1.75
- standardize_shift: float32 [256], replicated, may hold values from -3 to 3
- first_map_matrix: bfloat16 [256, 32], replicated, may hold values from -0.375 to 0.375
- first_map_intercept: float32 [32], replicated, may hold values from -3 to 3
- other_map_matrix: bfloat16 [256, 32], replicated, may hold values from -0.375 to 0.375
- other_map_intercept: float32 [32], replicated, may hold values from -3 to 3
- final_map_matrix: bfloat16 [1024, 128], replicated, may hold values from -0.1875 to 0.1875
- final_map_intercept: float32 [128], replicated, may hold values from -3 to 3
- coverage_lengths: int32 [6144], P('res'), may hold values from 0 to 256
- couple_features: float32 [6144, 216, 128], P('res'), may hold values from -6 to 6
Outputs:
- pair_out: float32 [6144, 216, 128], P('res')
All inputs are finite; a program needn't handle non-finite values.
Results may differ from a plain program's by a relative error of at most 0.0035.
Values may be sent and summed in bfloat16 or wider, within the bound.
No kernel may reach another device: no remote copies, remote signals or barrier semaphores. Data moves between devices by JAX's collectives and lax.ppermute only.
A program may use at most 128 MiB of HBM per device.

v0:
```python
import jax
import jax.numpy as jnp
from jax import lax
from jax.sharding import PartitionSpec as P

WIN = 4


def passed_along(array, axis, by):
    count = lax.axis_size(axis)
    pairs = [(i, i + by) for i in range(count) if 0 <= i + by < count]
    return lax.ppermute(array, axis, pairs)


def projected_row_values(
    homolog_lines,
    depth_row_slices,
    standardize_scale,
    standardize_shift,
    first_map_matrix,
    first_map_intercept,
    other_map_matrix,
    other_map_intercept,
):
    value_entries = homolog_lines.astype(jnp.float32)
    average = jnp.mean(value_entries, axis=-1, keepdims=True)
    centred = value_entries - average
    variance = jnp.mean(centred * centred, axis=-1, keepdims=True)
    normed = (centred * lax.rsqrt(variance + 1e-05) * standardize_scale + standardize_shift).astype(
        jnp.bfloat16
    )
    seq_index = jnp.arange(value_entries.shape[0], dtype=jnp.int32)
    seq_mask = (seq_index[:, None] < depth_row_slices[None, :]).astype(jnp.float32)[:, :, None]
    left_proj = (
        (
            jnp.dot(normed, first_map_matrix, preferred_element_type=jnp.float32)
            + first_map_intercept
        )
        * seq_mask
    ).astype(jnp.bfloat16)
    right_proj = (
        (
            jnp.dot(normed, other_map_matrix, preferred_element_type=jnp.float32)
            + other_map_intercept
        )
        * seq_mask
    ).astype(jnp.bfloat16)
    return (jnp.transpose(left_proj, (1, 2, 0)), jnp.transpose(right_proj, (1, 2, 0)))


def form_tile(
    left_rows, right_cols, depth_row_slices, depth_cols, final_map_matrix, final_map_intercept
):
    row_count, width, seq_count = left_rows.shape
    col_count = right_cols.shape[0]
    left_flat = left_rows.reshape(row_count * width, seq_count)
    right_flat = right_cols.reshape(col_count * width, seq_count)
    outer_sum = lax.dot_general(
        left_flat, right_flat, (((1,), (1,)), ((), ())), preferred_element_type=jnp.float32
    )
    outer_half = outer_sum.astype(jnp.bfloat16).reshape(row_count, width, col_count, width)
    weight_cube = final_map_matrix.reshape(width, width, final_map_matrix.shape[1])
    projected = (
        lax.dot_general(
            outer_half,
            weight_cube,
            (((1, 3), (0, 1)), ((), ())),
            preferred_element_type=jnp.float32,
        )
        + final_map_intercept
    )
    pair_count = jnp.maximum(
        jnp.minimum(
            depth_row_slices.astype(jnp.float32)[:, None], depth_cols.astype(jnp.float32)[None, :]
        ),
        1.0,
    )
    return projected / pair_count[:, :, None]


def on_device(
    homolog_features,
    standardize_scale,
    standardize_shift,
    first_map_matrix,
    first_map_intercept,
    other_map_matrix,
    other_map_intercept,
    final_map_matrix,
    final_map_intercept,
    coverage_lengths,
    couple_features,
):
    left_own, right_own = projected_row_values(
        homolog_features,
        coverage_lengths,
        standardize_scale,
        standardize_shift,
        first_map_matrix,
        first_map_intercept,
        other_map_matrix,
        other_map_intercept,
    )
    depth_own = coverage_lengths.astype(jnp.bfloat16)
    band_tiles = [None] * (2 * WIN + 1)
    band_tiles[WIN] = form_tile(
        left_own, right_own, depth_own, depth_own, final_map_matrix, final_map_intercept
    )
    for distance in range(1, WIN + 1):
        right_above, depth_above = passed_along((right_own, depth_own), "res", distance)
        band_tiles[WIN - distance] = form_tile(
            left_own, right_above, depth_own, depth_above, final_map_matrix, final_map_intercept
        )
        right_below, depth_below = passed_along((right_own, depth_own), "res", -distance)
        band_tiles[WIN + distance] = form_tile(
            left_own, right_below, depth_own, depth_below, final_map_matrix, final_map_intercept
        )
    block_index = lax.axis_index("res")
    block_total = lax.axis_size("res")
    pieces = []
    for offset in range(2 * WIN + 1):
        column_block = block_index + (offset - WIN)
        inside = (column_block >= 0) & (column_block < block_total)
        pieces.append(jnp.where(inside, band_tiles[offset], 0.0))
    return couple_features + jnp.concatenate(pieces, axis=1)


def solution(mesh):
    return jax.shard_map(
        on_device,
        mesh=mesh,
        in_specs=(
            P(None, "res", None),
            P(),
            P(),
            P(),
            P(),
            P(),
            P(),
            P(),
            P(),
            P("res"),
            P("res", None, None),
        ),
        out_specs=P("res", None, None),
        check_vma=False,
    )
```

profile of v0, /device:TPU:6, one launch (start us, length us, event | category | flops | bytes accessed | tf_op | source)
XLA Modules:
  0.0 167.8 jit_solution(17759248057566644442)
XLA Ops:
  0.0 0.8 convert_convert_fusion
  0.8 3.9 %collective-permute-start.5 = (bf16[24]{0:T(256)(128)(2,1)S(1)}, bf16[24]{0:T(256)(128)(2,1)}, u32[]{:S(2)}, u32[]{:S(2)}) collective-permute-start(bf16[24]{0:T(256)(128)(2,1)S(1)} %get-tuple-element.17), channel_id=1, source_target_pairs={{0,2},{1,3},{2,4},{3,5},{4,6},{5,7},{6,8},{7,9},{8,10},{9,11},{10,... | collective-permute-start | bytes 152 | tf_op jit(solution)/shard_map/ppermute | solution.py:12
  4.8 1.9 %collective-permute-start.7 = (bf16[24]{0:T(256)(128)(2,1)S(1)}, bf16[24]{0:T(256)(128)(2,1)}, u32[]{:S(2)}, u32[]{:S(2)}) collective-permute-start(bf16[24]{0:T(256)(128)(2,1)S(1)} %get-tuple-element.17), channel_id=1, source_target_pairs={{0,1},{1,2},{2,3},{3,4},{4,5},{5,6},{6,7},{7,8},{8,9},{9,10},{10,1... | collective-permute-start | bytes 152 | tf_op jit(solution)/shard_map/ppermute | solution.py:12
  6.7 8.0 %collective-permute-start.9 = (bf16[24]{0:T(256)(128)(2,1)S(1)}, bf16[24]{0:T(256)(128)(2,1)}, u32[]{:S(2)}, u32[]{:S(2)}) collective-permute-start(bf16[24]{0:T(256)(128)(2,1)S(1)} %get-tuple-element.17), channel_id=1, source_target_pairs={{1,0},{2,1},{3,2},{4,3},{5,4},{6,5},{7,6},{8,7},{9,8},{10,9},{11,1... | collective-permute-start | bytes 152 | tf_op jit(solution)/shard_map/ppermute | solution.py:12
  14.7 4.2 %collective-permute-start.11 = (bf16[24]{0:T(256)(128)(2,1)S(1)}, bf16[24]{0:T(256)(128)(2,1)}, u32[]{:S(2)}, u32[]{:S(2)}) collective-permute-start(bf16[24]{0:T(256)(128)(2,1)S(1)} %get-tuple-element.17), channel_id=1, source_target_pairs={{2,0},{3,1},{4,2},{5,3},{6,4},{7,5},{8,6},{9,7},{10,8},{11,9},{12,... | collective-permute-start | bytes 152 | tf_op jit(solution)/shard_map/ppermute | solution.py:12
  18.9 1.3 fusion.24
  20.3 2.8 %convert_reduce_fusion = f32[256,24]{1,0:T(8,128)S(1)} fusion(bf16[256,24,256]{2,1,0:T(8,128)(2,1)} %param.11), kind=kLoop, calls=%fused_computation.1 | loop fusion | flops 3139584 | bytes 3170304 | tf_op jit(solution)/shard_map/reduce_sum | solution.py:26
  23.1 1.8 %fusion.2 = f32[256,24]{1,0:T(8,128)S(1)} fusion(bf16[256,24,256]{2,1,0:T(8,128)(2,1)S(1)} %copy-done.1, f32[256,24]{1,0:T(8,128)S(1)} %broadcast_multiply_fusion), kind=kLoop, calls=%fused_computation.4 | loop fusion | flops 6285312 | bytes 3194880 | tf_op jit(solution)/shard_map/reduce_sum | solution.py:28
  25.0 0.7 copy-done.8
  25.6 3.8 %fusion.8 = f32[256,24,32]{2,1,0:T(8,128)} fusion(bf16[256,24,256]{2,1,0:T(8,128)(2,1)S(1)} %copy-done.1, f32[256]{0:T(256)S(1)} %copy-done.13, f32[256]{0:T(256)S(1)} %copy-done.14, f32[256,24]{1,0:T(8,128)S(1)} %add_rsqrt_fusion, f32[256,24]{1,0:T(8,128)S(1)} %broadcast_multiply_fusion, bf16[256,32]{0,1:T(8,128)(2,1)S(1)} %copy-done.12), kind=kOutput, calls=%fused_computation.18 | convolution fusion | flops 110100480 | bytes 3999744 | tf_op jit(solution)/shard_map/dot_general | solution.py:36
  29.4 3.1 %copy.15 = f32[256,24,32]{0,2,1:T(8,128)} copy(f32[256,24,32]{2,1,0:T(8,128)} %fusion.8) | data formatting | bytes 1572864 | tf_op jit(solution)/shard_map/dot_general | solution.py:36
  32.5 4.6 %fusion.6 = f32[256,24,32]{2,1,0:T(8,128)} fusion(bf16[256,24,256]{2,1,0:T(8,128)(2,1)S(1)} %copy-done.1, f32[256]{0:T(256)S(1)} %copy-done.13, f32[256]{0:T(256)S(1)} %copy-done.14, f32[256,24]{1,0:T(8,128)} %copy-done.8, f32[256,24]{1,0:T(8,128)S(1)} %broadcast_multiply_fusion, bf16[256,32]{0,1:T(8,128)(2,1)} %param.16), kind=kOutput, calls=%fused_computation.17 | convolution fusion | flops 110100480 | bytes 3999744 | tf_op jit(solution)/shard_map/dot_general | solution.py:43
  37.1 2.4 %copy.17 = f32[256,24,32]{0,2,1:T(8,128)S(1)} copy(f32[256,24,32]{2,1,0:T(8,128)} %fusion.6) | data formatting | bytes 1572864 | tf_op jit(solution)/shard_map/dot_general | solution.py:43
  39.6 0.3 fusion.22
  39.9 1.9 %collective-permute-start = (bf16[24,32,256]{2,1,0:T(8,128)(2,1)S(1)}, bf16[24,32,256]{2,1,0:T(8,128)(2,1)S(1)}, u32[]{:S(2)}, u32[]{:S(2)}) collective-permute-start(bf16[24,32,256]{2,1,0:T(8,128)(2,1)S(1)} %get-tuple-element.5), channel_id=1, source_target_pairs={{0,4},{1,5},{2,6},{3,7},{4,8},{5,9},{6,10},{7,11},{8,12},{9,13},{1... | collective-permute-start | bytes 1179656 | tf_op jit(solution)/shard_map/ppermute | solution.py:12
  41.8 0.5 convolution_convert_fusion.4
  42.3 4.5 %reshape.359 = bf16[24,32,24,32]{3,2,1,0:T(8,128)(2,1)} reshape(bf16[768,768]{1,0:T(8,128)(2,1)S(1)} %convolution_convert_fusion.4) | data formatting | bytes 2359296 | tf_op jit(solution)/shard_map/reshape | solution.py:61
  46.9 6.8 %collective-permute-start.13 = (bf16[24]{0:T(256)(128)(2,1)S(1)}, bf16[24]{0:T(256)(128)(2,1)S(1)}, u32[]{:S(2)}, u32[]{:S(2)}) collective-permute-start(bf16[24]{0:T(256)(128)(2,1)S(1)} %get-tuple-element.17), channel_id=1, source_target_pairs={{3,0},{4,1},{5,2},{6,3},{7,4},{8,5},{9,6},{10,7},{11,8},{12,9},{13... | collective-permute-start | bytes 152 | tf_op jit(solution)/shard_map/ppermute | solution.py:12
  53.7 0.7 convert_element_type.100
  54.4 4.1 %collective-permute-start.15 = (bf16[24]{0:T(256)(128)(2,1)S(1)}, bf16[24]{0:T(256)(128)(2,1)S(1)}, u32[]{:S(2)}, u32[]{:S(2)}) collective-permute-start(bf16[24]{0:T(256)(128)(2,1)S(1)} %get-tuple-element.17), channel_id=1, source_target_pairs={{4,0},{5,1},{6,2},{7,3},{8,4},{9,5},{10,6},{11,7},{12,8},{13,9},{1... | collective-permute-start | bytes 152 | tf_op jit(solution)/shard_map/ppermute | solution.py:12
  58.5 0.6 convert_element_type.102
  59.1 2.6 %collective-permute-start.1 = (bf16[24]{0:T(256)(128)(2,1)S(1)}, bf16[24]{0:T(256)(128)(2,1)S(1)}, u32[]{:S(2)}, u32[]{:S(2)}) collective-permute-start(bf16[24]{0:T(256)(128)(2,1)S(1)} %get-tuple-element.17), channel_id=1, source_target_pairs={{0,4},{1,5},{2,6},{3,7},{4,8},{5,9},{6,10},{7,11},{8,12},{9,13},{1... | collective-permute-start | bytes 152 | tf_op jit(solution)/shard_map/ppermute | solution.py:12
  61.7 0.7 convert_element_type.105
  62.4 2.6 %collective-permute-start.3 = (bf16[24]{0:T(256)(128)(2,1)S(1)}, bf16[24]{0:T(256)(128)(2,1)S(1)}, u32[]{:S(2)}, u32[]{:S(2)}) collective-permute-start(bf16[24]{0:T(256)(128)(2,1)S(1)} %get-tuple-element.17), channel_id=1, source_target_pairs={{0,3},{1,4},{2,5},{3,6},{4,7},{5,8},{6,9},{7,10},{8,11},{9,12},{10... | collective-permute-start | bytes 152 | tf_op jit(solution)/shard_map/ppermute | solution.py:12
  65.0 0.6 convert_element_type.107
  65.6 1.9 %collective-permute-start.2 = (bf16[24,32,256]{2,1,0:T(8,128)(2,1)S(1)}, bf16[24,32,256]{2,1,0:T(8,128)(2,1)S(1)}, u32[]{:S(2)}, u32[]{:S(2)}) collective-permute-start(bf16[24,32,256]{2,1,0:T(8,128)(2,1)S(1)} %get-tuple-element.5), channel_id=1, source_target_pairs={{0,3},{1,4},{2,5},{3,6},{4,7},{5,8},{6,9},{7,10},{8,11},{9,12},{10... | collective-permute-start | bytes 1179656 | tf_op jit(solution)/shard_map/ppermute | solution.py:12
  67.6 1.9 %collective-permute-start.4 = (bf16[24,32,256]{2,1,0:T(8,128)(2,1)S(1)}, bf16[24,32,256]{2,1,0:T(8,128)(2,1)S(1)}, u32[]{:S(2)}, u32[]{:S(2)}) collective-permute-start(bf16[24,32,256]{2,1,0:T(8,128)(2,1)S(1)} %get-tuple-element.5), channel_id=1, source_target_pairs={{0,2},{1,3},{2,4},{3,5},{4,6},{5,7},{6,8},{7,9},{8,10},{9,11},{10,... | collective-permute-start | bytes 1179656 | tf_op jit(solution)/shard_map/ppermute | solution.py:12
  69.5 0.1 collective-permute-done.1
  69.6 1.9 %collective-permute-start.6 = (bf16[24,32,256]{2,1,0:T(8,128)(2,1)S(1)}, bf16[24,32,256]{2,1,0:T(8,128)(2,1)S(1)}, u32[]{:S(2)}, u32[]{:S(2)}) collective-permute-start(bf16[24,32,256]{2,1,0:T(8,128)(2,1)S(1)} %get-tuple-element.5), channel_id=1, source_target_pairs={{0,1},{1,2},{2,3},{3,4},{4,5},{5,6},{6,7},{7,8},{8,9},{9,10},{10,1... | collective-permute-start | bytes 1179656 | tf_op jit(solution)/shard_map/ppermute | solution.py:12
  71.6 0.8 collective-permute-done.3
  72.4 7.0 %collective-permute-start.8 = (bf16[24,32,256]{2,1,0:T(8,128)(2,1)S(1)}, bf16[24,32,256]{2,1,0:T(8,128)(2,1)S(1)}, u32[]{:S(2)}, u32[]{:S(2)}) collective-permute-start(bf16[24,32,256]{2,1,0:T(8,128)(2,1)S(1)} %get-tuple-element.5), channel_id=1, source_target_pairs={{1,0},{2,1},{3,2},{4,3},{5,4},{6,5},{7,6},{8,7},{9,8},{10,9},{11,1... | collective-permute-start | bytes 1179656 | tf_op jit(solution)/shard_map/ppermute | solution.py:12
  79.4 0.1 minimum_maximum_fusion
  79.5 3.8 %collective-permute-start.10 = (bf16[24,32,256]{2,1,0:T(8,128)(2,1)S(1)}, bf16[24,32,256]{2,1,0:T(8,128)(2,1)S(1)}, u32[]{:S(2)}, u32[]{:S(2)}) collective-permute-start(bf16[24,32,256]{2,1,0:T(8,128)(2,1)S(1)} %get-tuple-element.5), channel_id=1, source_target_pairs={{2,0},{3,1},{4,2},{5,3},{6,4},{7,5},{8,6},{9,7},{10,8},{11,9},{12,... | collective-permute-start | bytes 1179656 | tf_op jit(solution)/shard_map/ppermute | solution.py:12
  83.4 0.5 convolution_convert_fusion.8
  83.9 4.1 %collective-permute-done.2 = bf16[24,32,256]{2,1,0:T(8,128)(2,1)S(1)} collective-permute-done((bf16[24,32,256]{2,1,0:T(8,128)(2,1)S(1)}, bf16[24,32,256]{2,1,0:T(8,128)(2,1)S(1)}, u32[]{:S(2)}, u32[]{:S(2)}) %collective-permute-start.2) | collective-permute-done | bytes 393248 | tf_op jit(solution)/shard_map/ppermute | solution.py:12
  88.0 2.8 %collective-permute-start.12 = (bf16[24,32,256]{2,1,0:T(8,128)(2,1)S(1)}, bf16[24,32,256]{2,1,0:T(8,128)(2,1)}, u32[]{:S(2)}, u32[]{:S(2)}) collective-permute-start(bf16[24,32,256]{2,1,0:T(8,128)(2,1)S(1)} %get-tuple-element.5), channel_id=1, source_target_pairs={{3,0},{4,1},{5,2},{6,3},{7,4},{8,5},{9,6},{10,7},{11,8},{12,9},{13... | collective-permute-start | bytes 1179656 | tf_op jit(solution)/shard_map/ppermute | solution.py:12
  90.8 0.5 convolution_convert_fusion.7
  91.3 4.0 %collective-permute-done.4 = bf16[24,32,256]{2,1,0:T(8,128)(2,1)S(1)} collective-permute-done((bf16[24,32,256]{2,1,0:T(8,128)(2,1)S(1)}, bf16[24,32,256]{2,1,0:T(8,128)(2,1)S(1)}, u32[]{:S(2)}, u32[]{:S(2)}) %collective-permute-start.4) | collective-permute-done | bytes 393248 | tf_op jit(solution)/shard_map/ppermute | solution.py:12
  95.4 4.9 %collective-permute-start.14 = (bf16[24,32,256]{2,1,0:T(8,128)(2,1)S(1)}, bf16[24,32,256]{2,1,0:T(8,128)(2,1)}, u32[]{:S(2)}, u32[]{:S(2)}) collective-permute-start(bf16[24,32,256]{2,1,0:T(8,128)(2,1)S(1)} %get-tuple-element.5), channel_id=1, source_target_pairs={{4,0},{5,1},{6,2},{7,3},{8,4},{9,5},{10,6},{11,7},{12,8},{13,9},{1... | collective-permute-start | bytes 1179656 | tf_op jit(solution)/shard_map/ppermute | solution.py:12
  100.3 1.5 convolution_convert_fusion.6
  101.9 1.6 convolution_convert_fusion.5
  103.5 1.6 convolution_convert_fusion.3
  105.1 1.6 convolution_convert_fusion.2
  106.7 4.5 %reshape.350 = bf16[24,32,24,32]{3,2,1,0:T(8,128)(2,1)} reshape(bf16[768,768]{1,0:T(8,128)(2,1)S(1)} %convolution_convert_fusion.8) | data formatting | bytes 2359296 | tf_op jit(solution)/shard_map/reshape | solution.py:61
  111.2 4.5 %reshape.353 = bf16[24,32,24,32]{3,2,1,0:T(8,128)(2,1)} reshape(bf16[768,768]{1,0:T(8,128)(2,1)S(1)} %convolution_convert_fusion.7) | data formatting | bytes 2359296 | tf_op jit(solution)/shard_map/reshape | solution.py:61
  115.6 4.5 %reshape.355 = bf16[24,32,24,32]{3,2,1,0:T(8,128)(2,1)} reshape(bf16[768,768]{1,0:T(8,128)(2,1)S(1)} %copy-done.2) | data formatting | bytes 2359296 | tf_op jit(solution)/shard_map/reshape | solution.py:61
  120.1 4.4 %reshape.357 = bf16[24,32,24,32]{3,2,1,0:T(8,128)(2,1)} reshape(bf16[768,768]{1,0:T(8,128)(2,1)S(1)} %copy-done.3) | data formatting | bytes 2359296 | tf_op jit(solution)/shard_map/reshape | solution.py:61
  124.5 4.5 %reshape.361 = bf16[24,32,24,32]{3,2,1,0:T(8,128)(2,1)} reshape(bf16[768,768]{1,0:T(8,128)(2,1)S(1)} %copy-done.4) | data formatting | bytes 2359296 | tf_op jit(solution)/shard_map/reshape | solution.py:61
  129.1 4.5 %reshape.363 = bf16[24,32,24,32]{3,2,1,0:T(8,128)(2,1)} reshape(bf16[768,768]{1,0:T(8,128)(2,1)S(1)} %copy-done.5) | data formatting | bytes 2359296 | tf_op jit(solution)/shard_map/reshape | solution.py:61
  133.6 1.5 convolution_convert_fusion.1
  135.1 4.5 %reshape.365 = bf16[24,32,24,32]{3,2,1,0:T(8,128)(2,1)} reshape(bf16[768,768]{1,0:T(8,128)(2,1)S(1)} %convolution_convert_fusion.1) | data formatting | bytes 2359296 | tf_op jit(solution)/shard_map/reshape | solution.py:61
  139.5 1.5 convolution_convert_fusion
  141.1 4.5 %reshape.367 = bf16[24,32,24,32]{3,2,1,0:T(8,128)(2,1)} reshape(bf16[768,768]{1,0:T(8,128)(2,1)S(1)} %convolution_convert_fusion) | data formatting | bytes 2359296 | tf_op jit(solution)/shard_map/reshape | solution.py:61
  145.5 3.8 %select_dynamic-update-slice_fusion.7 = f32[24,216,128]{2,1,0:T(8,128)S(1)} fusion(f32[24,24]{1,0:T(8,128)S(1)} %get-tuple-element.15, f32[128]{0:T(128)S(1)} %copy-done.15, bf16[24,32,24,32]{3,2,1,0:T(8,128)(2,1)} %reshape.350, bf16[32,32,128,1]{2,1,0,3:T(8,128)(2,1)S(1)} %bitcast.130, pred[]{:T(512)S(6)} %and.28), kind=kOutput, calls=%fused_computation.51 | convolution fusion | flops 151216128 | bytes 1739521 | tf_op jit(solution)/shard_map/dot_general | solution.py:64
  149.4 3.8 %select_dynamic-update-slice_fusion.6 = f32[24,216,128]{2,1,0:T(8,128)S(1)} fusion(f32[24,216,128]{2,1,0:T(8,128)S(1)} %select_dynamic-update-slice_fusion.7, f32[24,24]{1,0:T(8,128)S(1)} %get-tuple-element.8, f32[128]{0:T(128)S(1)} %copy-done.15, bf16[24,32,24,32]{3,2,1,0:T(8,128)(2,1)} %reshape.353, bf16[32,32,128,1]{2,1,0,3:T(8,128)(2,1)S(1)} %bitcast.131, ...), kind=kOutput, calls=%fused_computation.50 | convolution fusion | flops 151216128 | bytes 1749505 | tf_op jit(solution)/shard_map/dot_general | solution.py:64
  153.2 3.8 %select_dynamic-update-slice_fusion.5 = f32[24,216,128]{2,1,0:T(8,128)S(1)} fusion(f32[24,216,128]{2,1,0:T(8,128)S(1)} %select_dynamic-update-slice_fusion.6, f32[24,24]{1,0:T(8,128)S(1)} %get-tuple-element.9, f32[128]{0:T(128)S(1)} %copy-done.15, bf16[24,32,24,32]{3,2,1,0:T(8,128)(2,1)} %reshape.355, bf16[32,32,128,1]{2,1,0,3:T(8,128)(2,1)S(1)} %bitcast.132, ...), kind=kOutput, calls=%fused_computation.49 | convolution fusion | flops 151216128 | bytes 1749505 | tf_op jit(solution)/shard_map/dot_general | solution.py:64
  157.0 1.4 select_dynamic-update-slice_fusion.4
  158.4 1.4 fusion.21
  159.9 1.4 select_dynamic-update-slice_fusion.3
  161.3 1.4 select_dynamic-update-slice_fusion.2
  162.7 1.4 select_dynamic-update-slice_fusion.1
  164.2 1.4 select_dynamic-update-slice_fusion
  165.6 0.3 copy-done.7
  165.9 1.9 %add.154 = f32[24,216,128]{2,1,0:T(8,128)} add(f32[24,216,128]{2,1,0:T(8,128)S(1)} %copy-done.7, f32[24,216,128]{2,1,0:T(8,128)S(1)} %select_dynamic-update-slice_fusion) | non-fusion elementwise | flops 663552 | bytes 7962624 | tf_op jit(solution)/shard_map/add | solution.py:125
  (78 shorter events, 0.2 us)
Async XLA Ops:
  0.0 145.5 %copy-start = (bf16[1024,128]{1,0:T(8,128)(2,1)S(1)}, bf16[1024,128]{1,0:T(8,128)(2,1)}, u32[]{:S(2)}) copy-start(bf16[1024,128]{1,0:T(8,128)(2,1)} %param.18) | copy-start | bytes 786436
  0.0 23.1 %copy-start.1 = (bf16[256,24,256]{2,1,0:T(8,128)(2,1)S(1)}, bf16[256,24,256]{2,1,0:T(8,128)(2,1)}, u32[]{:S(2)}) copy-start(bf16[256,24,256]{2,1,0:T(8,128)(2,1)} %param.11) | copy-start | bytes 9437188
  0.8 46.0 %collective-permute-start.5 = (bf16[24]{0:T(256)(128)(2,1)S(1)}, bf16[24]{0:T(256)(128)(2,1)}, u32[]{:S(2)}, u32[]{:S(2)}) collective-permute-start(bf16[24]{0:T(256)(128)(2,1)S(1)} %get-tuple-element.17), channel_id=1, source_target_pairs={{0,2},{1,3},{2,4},{3,5},{4,6},{5,7},{6,8},{7,9},{8,10},{9,11},{10,... | collective-permute-start | bytes 152 | tf_op jit(solution)/shard_map/ppermute | solution.py:12
  4.8 49.6 %collective-permute-start.7 = (bf16[24]{0:T(256)(128)(2,1)S(1)}, bf16[24]{0:T(256)(128)(2,1)}, u32[]{:S(2)}, u32[]{:S(2)}) collective-permute-start(bf16[24]{0:T(256)(128)(2,1)S(1)} %get-tuple-element.17), channel_id=1, source_target_pairs={{0,1},{1,2},{2,3},{3,4},{4,5},{5,6},{6,7},{7,8},{8,9},{9,10},{10,1... | collective-permute-start | bytes 152 | tf_op jit(solution)/shard_map/ppermute | solution.py:12
  6.7 52.4 %collective-permute-start.9 = (bf16[24]{0:T(256)(128)(2,1)S(1)}, bf16[24]{0:T(256)(128)(2,1)}, u32[]{:S(2)}, u32[]{:S(2)}) collective-permute-start(bf16[24]{0:T(256)(128)(2,1)S(1)} %get-tuple-element.17), channel_id=1, source_target_pairs={{1,0},{2,1},{3,2},{4,3},{5,4},{6,5},{7,6},{8,7},{9,8},{10,9},{11,1... | collective-permute-start | bytes 152 | tf_op jit(solution)/shard_map/ppermute | solution.py:12
  14.7 47.7 %collective-permute-start.11 = (bf16[24]{0:T(256)(128)(2,1)S(1)}, bf16[24]{0:T(256)(128)(2,1)}, u32[]{:S(2)}, u32[]{:S(2)}) collective-permute-start(bf16[24]{0:T(256)(128)(2,1)S(1)} %get-tuple-element.17), channel_id=1, source_target_pairs={{2,0},{3,1},{4,2},{5,3},{6,4},{7,5},{8,6},{9,7},{10,8},{11,9},{12,... | collective-permute-start | bytes 152 | tf_op jit(solution)/shard_map/ppermute | solution.py:12
  20.3 5.4 %copy-start.12 = (bf16[256,32]{0,1:T(8,128)(2,1)S(1)}, bf16[256,32]{0,1:T(8,128)(2,1)}, u32[]{:S(2)}) copy-start(bf16[256,32]{0,1:T(8,128)(2,1)} %param.14) | copy-start | bytes 49156
  20.3 5.4 %copy-start.13 = (f32[256]{0:T(256)S(1)}, f32[256]{0:T(256)}, u32[]{:S(2)}) copy-start(f32[256]{0:T(256)} %param.13) | copy-start | bytes 3076
  20.3 5.4 %copy-start.14 = (f32[256]{0:T(256)S(1)}, f32[256]{0:T(256)}, u32[]{:S(2)}) copy-start(f32[256]{0:T(256)} %param.12) | copy-start | bytes 3076
  25.0 0.7 copy-start.8
  37.1 2.4 %copy-start.6 = (f32[256,24,32]{0,2,1:T(8,128)S(1)}, f32[256,24,32]{0,2,1:T(8,128)}, u32[]{:S(2)}) copy-start(f32[256,24,32]{0,2,1:T(8,128)} %copy.15) | copy-start | bytes 2359300
  37.1 2.4 %copy-start.9 = (f32[24,256]{1,0:T(8,128)S(1)}, f32[24,256]{1,0:T(8,128)}, u32[]{:S(2)}) copy-start(f32[24,256]{1,0:T(8,128)} %fusion.24) | copy-start | bytes 73732
  37.1 2.4 %copy-start.10 = (f32[32]{0:T(128)S(1)}, f32[32]{0:T(128)}, u32[]{:S(2)}) copy-start(f32[32]{0:T(128)} %param.17) | copy-start | bytes 388
  37.1 2.4 %copy-start.11 = (f32[32]{0:T(128)S(1)}, f32[32]{0:T(128)}, u32[]{:S(2)}) copy-start(f32[32]{0:T(128)} %param.15) | copy-start | bytes 388
  39.9 39.7 %collective-permute-start = (bf16[24,32,256]{2,1,0:T(8,128)(2,1)S(1)}, bf16[24,32,256]{2,1,0:T(8,128)(2,1)S(1)}, u32[]{:S(2)}, u32[]{:S(2)}) collective-permute-start(bf16[24,32,256]{2,1,0:T(8,128)(2,1)S(1)} %get-tuple-element.5), channel_id=1, source_target_pairs={{0,4},{1,5},{2,6},{3,7},{4,8},{5,9},{6,10},{7,11},{8,12},{9,13},{1... | collective-permute-start | bytes 1179656 | tf_op jit(solution)/shard_map/ppermute | solution.py:12
  46.9 18.8 %collective-permute-start.13 = (bf16[24]{0:T(256)(128)(2,1)S(1)}, bf16[24]{0:T(256)(128)(2,1)S(1)}, u32[]{:S(2)}, u32[]{:S(2)}) collective-permute-start(bf16[24]{0:T(256)(128)(2,1)S(1)} %get-tuple-element.17), channel_id=1, source_target_pairs={{3,0},{4,1},{5,2},{6,3},{7,4},{8,5},{9,6},{10,7},{11,8},{12,9},{13... | collective-permute-start | bytes 152 | tf_op jit(solution)/shard_map/ppermute | solution.py:12
  54.4 13.2 %collective-permute-start.15 = (bf16[24]{0:T(256)(128)(2,1)S(1)}, bf16[24]{0:T(256)(128)(2,1)S(1)}, u32[]{:S(2)}, u32[]{:S(2)}) collective-permute-start(bf16[24]{0:T(256)(128)(2,1)S(1)} %get-tuple-element.17), channel_id=1, source_target_pairs={{4,0},{5,1},{6,2},{7,3},{8,4},{9,5},{10,6},{11,7},{12,8},{13,9},{1... | collective-permute-start | bytes 152 | tf_op jit(solution)/shard_map/ppermute | solution.py:12
  59.1 10.5 %collective-permute-start.1 = (bf16[24]{0:T(256)(128)(2,1)S(1)}, bf16[24]{0:T(256)(128)(2,1)S(1)}, u32[]{:S(2)}, u32[]{:S(2)}) collective-permute-start(bf16[24]{0:T(256)(128)(2,1)S(1)} %get-tuple-element.17), channel_id=1, source_target_pairs={{0,4},{1,5},{2,6},{3,7},{4,8},{5,9},{6,10},{7,11},{8,12},{9,13},{1... | collective-permute-start | bytes 152 | tf_op jit(solution)/shard_map/ppermute | solution.py:12
  62.4 10.0 %collective-permute-start.3 = (bf16[24]{0:T(256)(128)(2,1)S(1)}, bf16[24]{0:T(256)(128)(2,1)S(1)}, u32[]{:S(2)}, u32[]{:S(2)}) collective-permute-start(bf16[24]{0:T(256)(128)(2,1)S(1)} %get-tuple-element.17), channel_id=1, source_target_pairs={{0,3},{1,4},{2,5},{3,6},{4,7},{5,8},{6,9},{7,10},{8,11},{9,12},{10... | collective-permute-start | bytes 152 | tf_op jit(solution)/shard_map/ppermute | solution.py:12
  65.6 22.3 %collective-permute-start.2 = (bf16[24,32,256]{2,1,0:T(8,128)(2,1)S(1)}, bf16[24,32,256]{2,1,0:T(8,128)(2,1)S(1)}, u32[]{:S(2)}, u32[]{:S(2)}) collective-permute-start(bf16[24,32,256]{2,1,0:T(8,128)(2,1)S(1)} %get-tuple-element.5), channel_id=1, source_target_pairs={{0,3},{1,4},{2,5},{3,6},{4,7},{5,8},{6,9},{7,10},{8,11},{9,12},{10... | collective-permute-start | bytes 1179656 | tf_op jit(solution)/shard_map/ppermute | solution.py:12
  67.6 27.8 %collective-permute-start.4 = (bf16[24,32,256]{2,1,0:T(8,128)(2,1)S(1)}, bf16[24,32,256]{2,1,0:T(8,128)(2,1)S(1)}, u32[]{:S(2)}, u32[]{:S(2)}) collective-permute-start(bf16[24,32,256]{2,1,0:T(8,128)(2,1)S(1)} %get-tuple-element.5), channel_id=1, source_target_pairs={{0,2},{1,3},{2,4},{3,5},{4,6},{5,7},{6,8},{7,9},{8,10},{9,11},{10,... | collective-permute-start | bytes 1179656 | tf_op jit(solution)/shard_map/ppermute | solution.py:12
  69.6 32.2 %collective-permute-start.6 = (bf16[24,32,256]{2,1,0:T(8,128)(2,1)S(1)}, bf16[24,32,256]{2,1,0:T(8,128)(2,1)S(1)}, u32[]{:S(2)}, u32[]{:S(2)}) collective-permute-start(bf16[24,32,256]{2,1,0:T(8,128)(2,1)S(1)} %get-tuple-element.5), channel_id=1, source_target_pairs={{0,1},{1,2},{2,3},{3,4},{4,5},{5,6},{6,7},{7,8},{8,9},{9,10},{10,1... | collective-permute-start | bytes 1179656 | tf_op jit(solution)/shard_map/ppermute | solution.py:12
  72.4 31.1 %collective-permute-start.8 = (bf16[24,32,256]{2,1,0:T(8,128)(2,1)S(1)}, bf16[24,32,256]{2,1,0:T(8,128)(2,1)S(1)}, u32[]{:S(2)}, u32[]{:S(2)}) collective-permute-start(bf16[24,32,256]{2,1,0:T(8,128)(2,1)S(1)} %get-tuple-element.5), channel_id=1, source_target_pairs={{1,0},{2,1},{3,2},{4,3},{5,4},{6,5},{7,6},{8,7},{9,8},{10,9},{11,1... | collective-permute-start | bytes 1179656 | tf_op jit(solution)/shard_map/ppermute | solution.py:12
  79.5 25.6 %collective-permute-start.10 = (bf16[24,32,256]{2,1,0:T(8,128)(2,1)S(1)}, bf16[24,32,256]{2,1,0:T(8,128)(2,1)S(1)}, u32[]{:S(2)}, u32[]{:S(2)}) collective-permute-start(bf16[24,32,256]{2,1,0:T(8,128)(2,1)S(1)} %get-tuple-element.5), channel_id=1, source_target_pairs={{2,0},{3,1},{4,2},{5,3},{6,4},{7,5},{8,6},{9,7},{10,8},{11,9},{12,... | collective-permute-start | bytes 1179656 | tf_op jit(solution)/shard_map/ppermute | solution.py:12
  88.0 45.6 %collective-permute-start.12 = (bf16[24,32,256]{2,1,0:T(8,128)(2,1)S(1)}, bf16[24,32,256]{2,1,0:T(8,128)(2,1)}, u32[]{:S(2)}, u32[]{:S(2)}) collective-permute-start(bf16[24,32,256]{2,1,0:T(8,128)(2,1)S(1)} %get-tuple-element.5), channel_id=1, source_target_pairs={{3,0},{4,1},{5,2},{6,3},{7,4},{8,5},{9,6},{10,7},{11,8},{12,9},{13... | collective-permute-start | bytes 1179656 | tf_op jit(solution)/shard_map/ppermute | solution.py:12
  95.4 44.2 %collective-permute-start.14 = (bf16[24,32,256]{2,1,0:T(8,128)(2,1)S(1)}, bf16[24,32,256]{2,1,0:T(8,128)(2,1)}, u32[]{:S(2)}, u32[]{:S(2)}) collective-permute-start(bf16[24,32,256]{2,1,0:T(8,128)(2,1)S(1)} %get-tuple-element.5), channel_id=1, source_target_pairs={{4,0},{5,1},{6,2},{7,3},{8,4},{9,5},{10,6},{11,7},{12,8},{13,9},{1... | collective-permute-start | bytes 1179656 | tf_op jit(solution)/shard_map/ppermute | solution.py:12
  111.2 4.5 %copy-start.2 = (bf16[768,768]{1,0:T(8,128)(2,1)S(1)}, bf16[768,768]{1,0:T(8,128)(2,1)}, u32[]{:S(2)}) copy-start(bf16[768,768]{1,0:T(8,128)(2,1)} %convolution_convert_fusion.6) | copy-start | bytes 3538948
  115.6 4.5 %copy-start.3 = (bf16[768,768]{1,0:T(8,128)(2,1)S(1)}, bf16[768,768]{1,0:T(8,128)(2,1)}, u32[]{:S(2)}) copy-start(bf16[768,768]{1,0:T(8,128)(2,1)} %convolution_convert_fusion.5) | copy-start | bytes 3538948
  120.1 4.4 %copy-start.4 = (bf16[768,768]{1,0:T(8,128)(2,1)S(1)}, bf16[768,768]{1,0:T(8,128)(2,1)}, u32[]{:S(2)}) copy-start(bf16[768,768]{1,0:T(8,128)(2,1)} %convolution_convert_fusion.3) | copy-start | bytes 3538948
  124.5 4.5 %copy-start.5 = (bf16[768,768]{1,0:T(8,128)(2,1)S(1)}, bf16[768,768]{1,0:T(8,128)(2,1)}, u32[]{:S(2)}) copy-start(bf16[768,768]{1,0:T(8,128)(2,1)} %convolution_convert_fusion.2) | copy-start | bytes 3538948
  141.0 4.5 %copy-start.15 = (f32[128]{0:T(128)S(1)}, f32[128]{0:T(128)}, u32[]{:S(2)}) copy-start(f32[128]{0:T(128)} %param.19) | copy-start | bytes 1540
  145.5 11.4 %slice-start.10 = ((s8[4718592]{0:T(1024)(128)(4,1)}), s8[4194304]{0:T(1024)(128)(4,1)S(1)}, s32[]{:S(2)}) async-start(s8[4718592]{0:T(1024)(128)(4,1)} %bitcast.158), calls=%async_computation.10 | async-start | bytes 8388608
  149.3 7.6 %slice-start.11 = ((s8[4718592]{0:T(1024)(128)(4,1)}), s8[524288]{0:T(1024)(128)(4,1)S(1)}, s32[]{:S(2)}) async-start(s8[4718592]{0:T(1024)(128)(4,1)} %bitcast.158), calls=%async_computation.11 | async-start | bytes 1048576
  149.3 9.0 %slice-start = ((s8[4718592]{0:T(1024)(128)(4,1)}), s8[4194304]{0:T(1024)(128)(4,1)S(1)}, s32[]{:S(2)}) async-start(s8[4718592]{0:T(1024)(128)(4,1)} %bitcast.148), calls=%async_computation | async-start | bytes 8388608
  153.1 5.3 %slice-start.1 = ((s8[4718592]{0:T(1024)(128)(4,1)}), s8[524288]{0:T(1024)(128)(4,1)S(1)}, s32[]{:S(2)}) async-start(s8[4718592]{0:T(1024)(128)(4,1)} %bitcast.148), calls=%async_computation.1 | async-start | bytes 1048576
  153.1 6.7 %slice-start.6 = ((s8[4718592]{0:T(1024)(128)(4,1)}), s8[4194304]{0:T(1024)(128)(4,1)S(1)}, s32[]{:S(2)}) async-start(s8[4718592]{0:T(1024)(128)(4,1)} %bitcast.154), calls=%async_computation.6 | async-start | bytes 8388608
  156.9 2.9 %slice-start.7 = ((s8[4718592]{0:T(1024)(128)(4,1)}), s8[524288]{0:T(1024)(128)(4,1)S(1)}, s32[]{:S(2)}) async-start(s8[4718592]{0:T(1024)(128)(4,1)} %bitcast.154), calls=%async_computation.7 | async-start | bytes 1048576
  157.0 4.3 %slice-start.2 = ((s8[4718592]{0:T(1024)(128)(4,1)}), s8[4194304]{0:T(1024)(128)(4,1)S(1)}, s32[]{:S(2)}) async-start(s8[4718592]{0:T(1024)(128)(4,1)} %bitcast.150), calls=%async_computation.2 | async-start | bytes 8388608
  158.4 2.9 %slice-start.3 = ((s8[4718592]{0:T(1024)(128)(4,1)}), s8[524288]{0:T(1024)(128)(4,1)S(1)}, s32[]{:S(2)}) async-start(s8[4718592]{0:T(1024)(128)(4,1)} %bitcast.150), calls=%async_computation.3 | async-start | bytes 1048576
  158.4 4.3 %slice-start.4 = ((s8[4718592]{0:T(1024)(128)(4,1)}), s8[4194304]{0:T(1024)(128)(4,1)S(1)}, s32[]{:S(2)}) async-start(s8[4718592]{0:T(1024)(128)(4,1)} %bitcast.152), calls=%async_computation.4 | async-start | bytes 8388608
  159.9 2.9 %slice-start.5 = ((s8[4718592]{0:T(1024)(128)(4,1)}), s8[524288]{0:T(1024)(128)(4,1)S(1)}, s32[]{:S(2)}) async-start(s8[4718592]{0:T(1024)(128)(4,1)} %bitcast.152), calls=%async_computation.5 | async-start | bytes 1048576
  159.9 4.3 %slice-start.8 = ((s8[4718592]{0:T(1024)(128)(4,1)}), s8[4194304]{0:T(1024)(128)(4,1)S(1)}, s32[]{:S(2)}) async-start(s8[4718592]{0:T(1024)(128)(4,1)} %bitcast.156), calls=%async_computation.8 | async-start | bytes 8388608
  161.3 2.9 %slice-start.9 = ((s8[4718592]{0:T(1024)(128)(4,1)}), s8[524288]{0:T(1024)(128)(4,1)S(1)}, s32[]{:S(2)}) async-start(s8[4718592]{0:T(1024)(128)(4,1)} %bitcast.156), calls=%async_computation.9 | async-start | bytes 1048576
  164.2 1.8 %copy-start.7 = (f32[24,216,128]{2,1,0:T(8,128)S(1)}, f32[24,216,128]{2,1,0:T(8,128)}, u32[]{:S(2)}) copy-start(f32[24,216,128]{2,1,0:T(8,128)} %param.21) | copy-start | bytes 7962628
where the time goes:
time: 169 us; the launch traced here: 168 us
  starting transfers between devices  60.6 us (36%)
  local copies, waits for them, and re-layouts  46.9 us (28%)
  matrix products  39 us (23%)
  other arithmetic  11.6 us (7%)
  waiting for transfers between devices  9.06 us (5%)
    ppermute x16, starting transfers between devices, passed_along(): return lax.ppermute(array, axis, pairs)  60.6 us
    reshape x9, local copies, waits for them, and re-layouts, form_tile(): outer_sum.astype(jnp.bfloat16).reshape(row_count, width, col_count, width)  40.3 us
    dot_general x9, matrix products, form_tile(): lax.dot_general(outer_half, weight_cube, (((1, 3), (0, 1)), ((), ())), pr...  19.7 us
    dot_general x9, matrix products, form_tile(): lax.dot_general(left_flat, right_flat, (((1,), (1,)), ((), ())), preferre...  10.9 us
    ppermute x16, waiting for transfers between devices, passed_along(): return lax.ppermute(array, axis, pairs)  9.06 us
    dot_general x1, matrix products, projected_row_values(): jnp.dot(normed, other_map_matrix, preferred_element_type=jnp.float32)  4.63 us
    dot_general x1, matrix products, projected_row_values(): jnp.dot(normed, first_map_matrix, preferred_element_type=jnp.float32)  3.77 us
  transfers between devices with their start and end apart: 16, of which 4 were waited for; matrix products, arithmetic and copies ran while one was open for 41% of the time, Pallas kernels for 0%

commit v1 on v0

v1 whole, which is shorter than its diff:
```python
import functools

import jax
import jax.numpy as jnp
from jax import lax
from jax.experimental import pallas as pl
from jax.experimental.pallas import tpu as pltpu
from jax.sharding import PartitionSpec as P

WIN = 4
ROWS = 24
WIDTH = 32
SEQS = 256
STEP = 32
FLAT = ROWS * WIDTH
SENT = FLAT + 16

BF16 = jnp.bfloat16
F32 = jnp.float32
NT = (((1,), (1,)), ((), ()))


def as_column(row, count):
    width = row.shape[1]
    wide = jnp.broadcast_to(row, (count, width))
    at = lax.broadcasted_iota(jnp.int32, (count, width), 1)
    down = lax.broadcasted_iota(jnp.int32, (count, width), 0)
    return jnp.sum(jnp.where(at == down, wide, 0.0), axis=1, keepdims=True)


def project_kernel(
    depth_ref,
    lines_ref,
    scale_ref,
    shift_ref,
    first_ref,
    first_bias_ref,
    other_ref,
    other_bias_ref,
    left_ref,
    right_ref,
    low_ref,
    high_ref,
    maps_ref,
    turn_ref,
    right_low_ref,
    right_high_ref,
):
    step = pl.program_id(0)
    scale = scale_ref[...]
    shift = shift_ref[...]
    part = 4
    for c in range(STEP // part):
        x = lines_ref[c * part : (c + 1) * part].astype(F32).reshape(part * ROWS, -1)
        centred = x - jnp.mean(x, axis=1, keepdims=True)
        variance = jnp.mean(centred * centred, axis=1, keepdims=True)
        normed = centred * lax.rsqrt(variance + 1e-05) * scale + shift
        at = pl.ds(pl.multiple_of((step * STEP + c * part) * ROWS, 8), part * ROWS)
        low_ref[at, :] = normed[:, :128]
        high_ref[at, :] = normed[:, 128:]

    @pl.when(step == SEQS // STEP - 1)
    def _():
        maps_ref[:WIDTH, :] = first_ref[...].astype(F32).T
        turned = other_ref[...].astype(F32).T
        first_bias = as_column(first_bias_ref[...], WIDTH)
        other_bias = jnp.broadcast_to(as_column(other_bias_ref[...], WIDTH), (WIDTH, 128))
        turn_ref[0] = turned[:, :128]
        turn_ref[1] = turned[:, 128:]
        turn_ref[2] = other_bias
        biases = [jnp.broadcast_to(first_bias, (WIDTH, 128))]
        for k in range(4):
            for half in range(2):
                maps_ref[WIDTH + 8 * k : WIDTH + 8 * k + 8, half * 128 : half * 128 + 128] = (
                    turn_ref[half, pl.ds(k, 8, stride=4), :]
                )
            biases.append(turn_ref[2, pl.ds(k, 8, stride=4), :])
        bias = jnp.concatenate(biases, axis=0)
        bias = jnp.concatenate([bias, bias], axis=1)
        maps = maps_ref[...].astype(BF16)
        seq = lax.broadcasted_iota(jnp.int32, (2 * WIDTH, SEQS), 1)
        lane = lax.broadcasted_iota(jnp.int32, (16, SEQS), 1)
        depths = jnp.zeros((16, SEQS), F32)
        for i in range(ROWS):
            depth = depth_ref[i]
            rows = jnp.concatenate(
                [low_ref[pl.ds(i, SEQS, stride=ROWS), :], high_ref[pl.ds(i, SEQS, stride=ROWS), :]],
                axis=1,
            ).astype(BF16)
            both = lax.dot_general(maps, rows, NT, preferred_element_type=F32) + bias
            both = jnp.where(seq < depth, both, 0.0)
            left_ref[i * WIDTH : (i + 1) * WIDTH, :] = both[:WIDTH].astype(BF16)
            right_low_ref[pl.ds(i, WIDTH, stride=ROWS), :] = both[WIDTH:, :128]
            right_high_ref[pl.ds(i, WIDTH, stride=ROWS), :] = both[WIDTH:, 128:]
            depths = jnp.where(lane == i, depth.astype(F32), depths)
        right_ref[:FLAT, :128] = right_low_ref[...].astype(BF16)
        right_ref[:FLAT, 128:] = right_high_ref[...].astype(BF16)
        right_ref[FLAT:, :] = depths.astype(BF16)


def whole(shape):
    return pl.BlockSpec(shape, lambda *_: (0,) * len(shape))


def project(lines, depth, scale, shift, first, first_bias, other, other_bias):
    channels = lines.shape[2]
    return pl.pallas_call(
        project_kernel,
        grid=(SEQS // STEP,),
        in_specs=[
            pl.BlockSpec(memory_space=pltpu.SMEM),
            pl.BlockSpec((STEP, ROWS, channels), lambda s: (s, 0, 0)),
            whole((1, channels)),
            whole((1, channels)),
            whole((channels, WIDTH)),
            whole((1, WIDTH)),
            whole((channels, WIDTH)),
            whole((1, WIDTH)),
        ],
        out_specs=[whole((FLAT, SEQS)), whole((SENT, SEQS))],
        out_shape=[
            jax.ShapeDtypeStruct((FLAT, SEQS), BF16),
            jax.ShapeDtypeStruct((SENT, SEQS), BF16),
        ],
        scratch_shapes=[
            pltpu.VMEM((SEQS * ROWS, 128), F32),
            pltpu.VMEM((SEQS * ROWS, 128), F32),
            pltpu.VMEM((2 * WIDTH, channels), F32),
            pltpu.VMEM((3, WIDTH, 128), F32),
            pltpu.VMEM((FLAT, 128), F32),
            pltpu.VMEM((FLAT, 128), F32),
        ],
        compiler_params=pltpu.CompilerParams(vmem_limit_bytes=40 << 20),
        cost_estimate=pl.CostEstimate(
            flops=2 * 6144 * 256 * 64, bytes_accessed=4 << 20, transcendentals=6144
        ),
        name="project",
    )(
        depth,
        lines,
        scale.reshape(1, -1),
        shift.reshape(1, -1),
        first,
        first_bias.reshape(1, -1),
        other,
        other_bias.reshape(1, -1),
    )


def tiles_kernel(count, fresh, *refs):
    place_ref, depth_ref, left_ref, *rest = refs
    right_refs, rest = rest[:count], rest[count:]
    final_ref, bias_ref, couple_ref, *rest = rest
    if not fresh:
        rest = rest[1:]
    out_ref, couple_buf, out_buf, take_sem, give_sem = rest

    def columns(b):
        return pl.ds(pl.multiple_of(place_ref[b] * ROWS, 8), ROWS)

    takes, gives = [], []
    for b in range(count):
        takes.append(
            pltpu.make_async_copy(couple_ref.at[:, columns(b), :], couple_buf.at[b], take_sem.at[b])
        )
        gives.append(
            pltpu.make_async_copy(out_buf.at[b], out_ref.at[:, columns(b), :], give_sem.at[b])
        )
        takes[-1].start()

    group = lax.broadcasted_iota(jnp.int32, (144, 128), 1) // WIDTH
    odd = (group & 1) == 1
    upper = (group & 2) == 2
    bias = bias_ref[...]

    def left_turned(k):
        return jnp.concatenate(
            [
                left_ref[(4 * h + (g ^ k)) * WIDTH : (4 * h + (g ^ k) + 1) * WIDTH, :]
                for h in range(6)
                for g in range(4)
            ],
            axis=0,
        )

    def final_turned(v):
        return jnp.concatenate(
            [
                final_ref[(4 * q + (g ^ v)) * WIDTH : (4 * q + (g ^ v) + 1) * WIDTH, :]
                for q in range(8)
                for g in range(4)
            ],
            axis=0,
        )

    for b in range(count):
        right = right_refs[b]
        parts = []
        for k in range(4):
            outer = lax.dot_general(
                right[k * 192 : (k + 1) * 192, :],
                left_turned(k),
                NT,
                preferred_element_type=F32,
            )
            parts.append(
                [
                    jnp.concatenate(
                        [
                            outer[q * ROWS : (q + 1) * ROWS, h * 128 : (h + 1) * 128]
                            for h in range(6)
                        ],
                        axis=0,
                    ).astype(BF16)
                    for q in range(8)
                ]
            )
        mixed = [[], [], [], []]
        for q in range(8):
            pair = [jnp.where(odd, parts[k ^ 1][q], parts[k][q]) for k in range(4)]
            for v in range(4):
                mixed[v].append(jnp.where(upper, pair[v ^ 2], pair[v]))
        depth_row = right[FLAT : FLAT + 16, :128].astype(F32)[:1, :]
        depth_cols = jnp.broadcast_to(as_column(depth_row, ROWS), (ROWS, 128))
        takes[b].wait()
        inside = place_ref[count + b].astype(F32)
        for v in range(4):
            sums = jnp.dot(
                jnp.concatenate(mixed[v], axis=1), final_turned(v), preferred_element_type=F32
            )
            for h in range(6):
                i = 4 * h + v
                pairs = jnp.maximum(jnp.minimum(depth_cols, depth_ref[i].astype(F32)), 1.0)
                update = (sums[h * ROWS : (h + 1) * ROWS] + bias) * (inside / pairs)
                out_buf[b, i] = couple_buf[b, i] + update
        gives[b].start()
    for b in range(count):
        gives[b].wait()


def form_tiles(places, depth, left, rights, final, final_bias, couple, out, name):
    count = len(rights)
    fresh = out is None
    vmem = pl.BlockSpec(memory_space=pltpu.VMEM)
    smem = pl.BlockSpec(memory_space=pltpu.SMEM)
    hbm = pl.BlockSpec(memory_space=pl.ANY)
    args = [places, depth, left, *rights, final, final_bias, couple]
    specs = [smem, smem, vmem] + [vmem] * count + [vmem, vmem, hbm]
    alias = {}
    if not fresh:
        alias = {len(args): 0}
        args.append(out)
        specs.append(hbm)
    return pl.pallas_call(
        functools.partial(tiles_kernel, count, fresh),
        in_specs=specs,
        out_specs=hbm,
        out_shape=jax.ShapeDtypeStruct(couple.shape, couple.dtype),
        input_output_aliases=alias,
        scratch_shapes=[
            pltpu.VMEM((count, ROWS, ROWS, 128), F32),
            pltpu.VMEM((count, ROWS, ROWS, 128), F32),
            pltpu.SemaphoreType.DMA((count,)),
            pltpu.SemaphoreType.DMA((count,)),
        ],
        compiler_params=pltpu.CompilerParams(vmem_limit_bytes=48 << 20),
        cost_estimate=pl.CostEstimate(
            flops=count * 2 * 576 * 1024 * (256 + 128),
            bytes_accessed=count * (2 * 294912 + 401408) + 700000,
            transcendentals=0,
        ),
        name=name,
    )(*args)


def on_device(
    homolog_features,
    standardize_scale,
    standardize_shift,
    first_map_matrix,
    first_map_intercept,
    other_map_matrix,
    other_map_intercept,
    final_map_matrix,
    final_map_intercept,
    coverage_lengths,
    couple_features,
):
    total = lax.axis_size("res")
    me = lax.axis_index("res")
    core = me % 2
    side = 1 - 2 * core

    def moved(block, by):
        return lax.ppermute(block, "res", [(i, (i + by) % total) for i in range(total)])

    def swapped(block):
        return lax.ppermute(block, "res", [(i, i ^ 1) for i in range(total)])

    left, own = project(
        homolog_features,
        coverage_lengths,
        standardize_scale,
        standardize_shift,
        first_map_matrix,
        first_map_intercept,
        other_map_matrix,
        other_map_intercept,
    )
    final = (
        final_map_matrix.reshape(WIDTH, WIDTH, -1).transpose(1, 0, 2).reshape(WIDTH * WIDTH, -1)
    )
    final_bias = final_map_intercept.reshape(1, -1)

    def tiles(distances, rights, out, name):
        at = jnp.stack([jnp.int32(d) + jnp.zeros((), jnp.int32) for d in distances])
        block = me + at
        inside = ((block >= 0) & (block < total)).astype(jnp.int32)
        places = jnp.concatenate([at + WIN, inside])
        return form_tiles(
            places, coverage_lengths, left, rights, final, final_bias, couple_features, out, name
        )

    below2 = moved(own, 2)
    above2 = moved(own, -2)
    sibling = swapped(own)
    out = tiles([0, side], [own, sibling], None, "near")
    below4 = moved(below2, 2)
    above4 = moved(above2, -2)
    below_odd = swapped(below2)
    above_odd = swapped(above2)
    out = tiles([-2, 2, side - 2, side + 2], [below2, above2, below_odd, above_odd], out, "middle")
    last = swapped(jnp.where(core == 0, above4, below4))
    out = tiles([-4, 4], [below4, above4], out, "far")
    return tiles([-3 * side], [last], out, "last")


def solution(mesh):
    return jax.shard_map(
        on_device,
        mesh=mesh,
        in_specs=(
            P(None, "res", None),
            P(),
            P(),
            P(),
            P(),
            P(),
            P(),
            P(),
            P(),
            P("res"),
            P("res", None, None),
        ),
        out_specs=P("res", None, None),
        check_vma=False,
    )
```

time: 169 us -> 77.9 us (0.46)
  the two profiles are of different devices: /device:TPU:6 before, /device:TPU:1 now
where the time goes in v1:
time: 77.9 us; the launch traced here: 77.6 us
  Pallas kernels  23 us (30%)
  starting transfers between devices  22.9 us (29%)
  waiting for transfers between devices  21.7 us (28%)
  local copies, waits for them, and re-layouts  8.1 us (10%)
  other arithmetic  1.59 us (2%)
    ppermute x4, waiting for transfers between devices, moved(): lax.ppermute(block, 'res', [(i, (i + by) % total) for i in range(total)])  21.7 us
    pallas_call x4, Pallas kernels, form_tiles(): pl.pallas_call(functools.partial(tiles_kernel, count, fresh), in_specs=sp...  16.8 us
    ppermute x4, starting transfers between devices, moved(): lax.ppermute(block, 'res', [(i, (i + by) % total) for i in range(total)])  16.1 us
    unnamed x22, local copies, waits for them, and re-layouts  7.04 us
    ppermute x4, starting transfers between devices, swapped(): return lax.ppermute(block, 'res', [(i, i ^ 1) for i in range(total)])  6.74 us
    pallas_call x1, Pallas kernels, project(): pl.pallas_call(project_kernel, grid=(SEQS // STEP,), in_specs=[pl.BlockSp...  6.22 us
  transfers between devices with their start and end apart: 8, of which 3 were waited for; matrix products, arithmetic and copies ran while one was open for 3% of the time, Pallas kernels for 18%

profile of v1, /device:TPU:1, one launch (start us, length us, event | category | flops | bytes accessed | tf_op | source)
XLA Modules:
  0.0 77.6 jit_solution(3097672414059060399)
XLA Ops:
  0.0 0.0 copy-start.9
  0.0 0.0 copy-start
  0.0 1.0 %copy.15.first_ref = bf16[256,32]{1,0:T(8,128)(2,1)S(1)} copy(bf16[256,32]{0,1:T(8,128)(2,1)} %param.14) | data formatting | bytes 32768 | tf_op args[3]
  1.0 0.8 %copy.16.other_ref = bf16[256,32]{1,0:T(8,128)(2,1)S(1)} copy(bf16[256,32]{0,1:T(8,128)(2,1)} %param.16) | data formatting | bytes 32768 | tf_op args[5]
  1.8 0.0 copy-start.1
  1.8 1.9 %copy-done.1 = bf16[256,24,256]{2,1,0:T(8,128)(2,1)S(1)} copy-done((bf16[256,24,256]{2,1,0:T(8,128)(2,1)S(1)}, bf16[256,24,256]{2,1,0:T(8,128)(2,1)}, u32[]{:S(2)}) %copy-start.1) | copy-done | bytes 3145752
  3.7 0.0 copy-start.2
  3.7 0.7 copy-done.2
  4.4 0.0 copy-start.5
  4.4 0.7 copy-done.5
  5.1 0.0 copy-start.6
  5.1 0.7 copy-done.6
  5.7 0.0 copy-start.7
  5.7 0.7 copy-done.7
  6.4 0.0 copy-start.8
  6.4 0.7 copy-done.8
  7.0 0.0 copy-start.3
  7.1 0.0 copy-start.4
  7.1 6.2 %project.1 = (bf16[768,256]{1,0:T(8,128)(2,1)S(1)}, bf16[784,256]{1,0:T(8,128)(2,1)}) custom-call(s32[24]{0:T(128)S(1)} %copy-done.2, bf16[256,24,256]{2,1,0:T(8,128)(2,1)S(1)} %copy-done.1, f32[1,256]{1,0:T(1,128)S(1)} %bitcast.22, f32[1,256]{1,0:T(1,128)S(1)} %bitcast.23, bf16[256,32]{1,0:T(8,128)(2,1)S(1)} %copy.15.first_ref, f32[1,32]{1,0:T(1,128)S(1)} %bitcast.24, ...), custom_call_target="tpu_custom_call" | custom-call | flops 201326592 | bytes 4194304 | tf_op jit(solution)/shard_map/project/pallas_call | solution.py:107
  13.3 3.2 %collective-permute-start.7 = (bf16[784,256]{1,0:T(8,128)(2,1)}, bf16[784,256]{1,0:T(8,128)(2,1)}, u32[]{:S(2)}, u32[]{:S(2)}) collective-permute-start(bf16[784,256]{1,0:T(8,128)(2,1)} %get-tuple-element.8.refs_3_), channel_id=1, source_target_pairs={{0,1},{1,0},{2,3},{3,2},{4,5},{5,4},{6,7},{7,6},{8,9},{9,8},{10,11... | collective-permute-start | bytes 1204232 | tf_op jit(solution)/shard_map/ppermute | solution.py:298
  16.5 0.0 collective-permute-start.2
  16.5 8.5 %collective-permute-start = (bf16[784,256]{1,0:T(8,128)(2,1)}, bf16[784,256]{1,0:T(8,128)(2,1)}, u32[]{:S(2)}, u32[]{:S(2)}) collective-permute-start(bf16[784,256]{1,0:T(8,128)(2,1)} %get-tuple-element.8.refs_3_), channel_id=1, source_target_pairs={{0,254},{1,255},{2,0},{3,1},{4,2},{5,3},{6,4},{7,5},{8,6},{9,7},{1... | collective-permute-start | bytes 1204232 | tf_op jit(solution)/shard_map/ppermute | solution.py:295
  25.0 0.1 and_convert_fusion
  25.1 0.1 broadcast_add_fusion
  25.2 0.1 pad_add_fusion.5.refs_0_
  25.2 0.1 broadcast_add_fusion.1
  25.3 8.7 %collective-permute-done.refs_4_ = bf16[784,256]{1,0:T(8,128)(2,1)} collective-permute-done((bf16[784,256]{1,0:T(8,128)(2,1)}, bf16[784,256]{1,0:T(8,128)(2,1)}, u32[]{:S(2)}, u32[]{:S(2)}) %collective-permute-start) | collective-permute-done | bytes 401440 | tf_op jit(solution)/shard_map/ppermute | solution.py:295
  34.0 7.6 %collective-permute-start.1 = (bf16[784,256]{1,0:T(8,128)(2,1)}, bf16[784,256]{1,0:T(8,128)(2,1)}, u32[]{:S(2)}, u32[]{:S(2)}) collective-permute-start(bf16[784,256]{1,0:T(8,128)(2,1)} %collective-permute-done.refs_4_), channel_id=1, source_target_pairs={{0,254},{1,255},{2,0},{3,1},{4,2},{5,3},{6,4},{7,5},{8,6},{9,7},{1... | collective-permute-start | bytes 1204232 | tf_op jit(solution)/shard_map/ppermute | solution.py:295
  41.7 0.0 collective-permute-done.2.refs_3_
  41.7 0.0 collective-permute-start.3
  41.7 0.1 pad_add_fusion.3.refs_0_
  41.7 0.0 copy-done.9
  41.8 0.1 pad_add_fusion.1.refs_0_
  41.8 1.1 %copy.17 = bf16[32,32,128]{2,0,1:T(8,128)(2,1)S(1)} copy(bf16[32,32,128]{2,1,0:T(8,128)(2,1)} %bitcast.26) | data formatting | bytes 524288 | tf_op jit(solution)/shard_map/reshape | solution.py:311
  42.9 1.2 %collective-permute-start.5 = (bf16[784,256]{1,0:T(8,128)(2,1)}, bf16[784,256]{1,0:T(8,128)(2,1)S(1)}, u32[]{:S(2)}, u32[]{:S(2)}) collective-permute-start(bf16[784,256]{1,0:T(8,128)(2,1)} %collective-permute-done.2.refs_3_), channel_id=1, source_target_pairs={{0,1},{1,0},{2,3},{3,2},{4,5},{5,4},{6,7},{7,6},{8,9},{9,8},{10,11... | collective-permute-start | bytes 1204232 | tf_op jit(solution)/shard_map/ppermute | solution.py:298
  44.1 0.1 collective-permute-start.6
  44.2 5.7 %collective-permute-done.1.refs_4_ = bf16[784,256]{1,0:T(8,128)(2,1)} collective-permute-done((bf16[784,256]{1,0:T(8,128)(2,1)}, bf16[784,256]{1,0:T(8,128)(2,1)}, u32[]{:S(2)}, u32[]{:S(2)}) %collective-permute-start.1) | collective-permute-done | bytes 401440 | tf_op jit(solution)/shard_map/ppermute | solution.py:295
  49.8 7.3 %collective-permute-done.3.refs_3_ = bf16[784,256]{1,0:T(8,128)(2,1)} collective-permute-done((bf16[784,256]{1,0:T(8,128)(2,1)}, bf16[784,256]{1,0:T(8,128)(2,1)}, u32[]{:S(2)}, u32[]{:S(2)}) %collective-permute-start.3) | collective-permute-done | bytes 401440 | tf_op jit(solution)/shard_map/ppermute | solution.py:295
  57.1 1.0 %broadcast_select_fusion = bf16[784,256]{1,0:T(8,128)(2,1)S(1)} fusion(bf16[784,256]{1,0:T(8,128)(2,1)} %collective-permute-done.1.refs_4_, bf16[784,256]{1,0:T(8,128)(2,1)} %collective-permute-done.3.refs_3_, pred[]{:T(512)S(6)} %eq.5), kind=kLoop, calls=%fused_computation | loop fusion | flops 200704 | bytes 1204225 | tf_op jit(solution)/shard_map/jit(_where)/select_n | solution.py:333
  58.2 2.3 %collective-permute-start.4 = (bf16[784,256]{1,0:T(8,128)(2,1)S(1)}, bf16[784,256]{1,0:T(8,128)(2,1)S(1)}, u32[]{:S(2)}, u32[]{:S(2)}) collective-permute-start(bf16[784,256]{1,0:T(8,128)(2,1)S(1)} %broadcast_select_fusion), channel_id=1, source_target_pairs={{0,1},{1,0},{2,3},{3,2},{4,5},{5,4},{6,7},{7,6},{8,9},{9,8},{10,11... | collective-permute-start | bytes 1204232 | tf_op jit(solution)/shard_map/ppermute | solution.py:298
  60.4 0.1 pad_add_fusion.refs_0_
  60.5 0.0 collective-permute-done.7.refs_4_
  60.5 0.0 copy-done
  60.5 0.0 copy-done.3
  60.5 0.0 copy-done.4
  60.5 4.1 %near.1.refs_10_ = f32[24,216,128]{2,1,0:T(8,128)} custom-call(s32[4]{0:T(128)S(1)} %pad_add_fusion.5.refs_0_, s32[24]{0:T(128)S(1)} %copy-done.3, bf16[768,256]{1,0:T(8,128)(2,1)S(1)} %get-tuple-element.7.refs_2_, bf16[784,256]{1,0:T(8,128)(2,1)} %get-tuple-element.8.refs_3_, bf16[784,256]{1,0:T(8,128)(2,1)} %collective-permute-done.7.refs_4_, ...), custom_call_target="tpu_custom_call" | custom-call | flops 905969664 | bytes 2682464 | tf_op jit(solution)/shard_map/near/pallas_call | solution.py:254
  64.6 0.0 collective-permute-done.5.refs_5_
  64.6 0.0 collective-permute-done.6.refs_6_
  64.6 6.2 %middle.1.refs_8_ = f32[24,216,128]{2,1,0:T(8,128)} custom-call(s32[8]{0:T(128)S(1)} %pad_add_fusion.3.refs_0_, s32[24]{0:T(128)S(1)} %copy-done.3, bf16[768,256]{1,0:T(8,128)(2,1)S(1)} %get-tuple-element.7.refs_2_, bf16[784,256]{1,0:T(8,128)(2,1)} %collective-permute-done.2.refs_3_, ...), custom_call_target="tpu_custom_call", output_to_operand_aliasing={{}: (10, {})} | custom-call | flops 1811939328 | bytes 4664928 | tf_op jit(solution)/shard_map/middle/pallas_call | solution.py:254
  70.8 4.1 %far.1.refs_7_ = f32[24,216,128]{2,1,0:T(8,128)} custom-call(s32[4]{0:T(128)S(1)} %pad_add_fusion.1.refs_0_, s32[24]{0:T(128)S(1)} %copy-done.3, bf16[768,256]{1,0:T(8,128)(2,1)S(1)} %get-tuple-element.7.refs_2_, bf16[784,256]{1,0:T(8,128)(2,1)} %collective-permute-done.3.refs_3_, ...), custom_call_target="tpu_custom_call", output_to_operand_aliasing={{}: (8, {})} | custom-call | flops 905969664 | bytes 2682464 | tf_op jit(solution)/shard_map/far/pallas_call | solution.py:254
  74.9 0.0 collective-permute-done.4.refs_3_
  74.9 2.5 %last.1 = f32[24,216,128]{2,1,0:T(8,128)} custom-call(s32[2]{0:T(128)S(1)} %pad_add_fusion.refs_0_, s32[24]{0:T(128)S(1)} %copy-done.3, bf16[768,256]{1,0:T(8,128)(2,1)S(1)} %get-tuple-element.7.refs_2_, bf16[784,256]{1,0:T(8,128)(2,1)S(1)} %collective-permute-done.4.refs_3_, bf16[1024,128]{1,0:T(8,128)(2,1)S(1)} %bitcast.17, ...), custom_call_target="tpu_custom_call", output_to_operand_aliasing={{}: (7, {})} | custom-call | flops 452984832 | bytes 1691232 | tf_op jit(solution)/shard_map/last/pallas_call | solution.py:254
  (3 shorter events, 0.0 us)
Async XLA Ops:
  0.0 41.7 %copy-start.9 = (s32[2]{0:T(128)S(1)}, s32[2]{0:T(128)}, u32[]{:S(2)}) copy-start(s32[2]{0:T(128)} %constant.44.clone.1) | copy-start | bytes 28
  0.0 60.5 %copy-start = (f32[24,216,128]{2,1,0:T(8,128)S(1)}, f32[24,216,128]{2,1,0:T(8,128)}, u32[]{:S(2)}) copy-start(f32[24,216,128]{2,1,0:T(8,128)} %refs_6_.1) | copy-start | bytes 7962628
  1.8 1.9 %copy-start.1 = (bf16[256,24,256]{2,1,0:T(8,128)(2,1)S(1)}, bf16[256,24,256]{2,1,0:T(8,128)(2,1)}, u32[]{:S(2)}) copy-start(bf16[256,24,256]{2,1,0:T(8,128)(2,1)} %lines_ref.1) | copy-start | bytes 9437188
  3.7 0.7 copy-start.2
  4.4 0.7 copy-start.5
  5.1 0.7 copy-start.6
  5.7 0.7 copy-start.7
  6.4 0.7 copy-start.8
  7.0 53.5 %copy-start.3 = (s32[24]{0:T(128)S(1)}, s32[24]{0:T(128)}, u32[]{:S(2)}) copy-start(s32[24]{0:T(128)} %refs_1_.7) | copy-start | bytes 292
  7.1 53.5 %copy-start.4 = (f32[128]{0:T(128)S(1)}, f32[128]{0:T(128)}, u32[]{:S(2)}) copy-start(f32[128]{0:T(128)} %param.19) | copy-start | bytes 1540
  13.3 47.2 %collective-permute-start.7 = (bf16[784,256]{1,0:T(8,128)(2,1)}, bf16[784,256]{1,0:T(8,128)(2,1)}, u32[]{:S(2)}, u32[]{:S(2)}) collective-permute-start(bf16[784,256]{1,0:T(8,128)(2,1)} %get-tuple-element.8.refs_3_), channel_id=1, source_target_pairs={{0,1},{1,0},{2,3},{3,2},{4,5},{5,4},{6,7},{7,6},{8,9},{9,8},{10,11... | collective-permute-start | bytes 1204232 | tf_op jit(solution)/shard_map/ppermute | solution.py:298
  16.5 25.2 %collective-permute-start.2 = (bf16[784,256]{1,0:T(8,128)(2,1)}, bf16[784,256]{1,0:T(8,128)(2,1)}, u32[]{:S(2)}, u32[]{:S(2)}) collective-permute-start(bf16[784,256]{1,0:T(8,128)(2,1)} %get-tuple-element.8.refs_3_), channel_id=1, source_target_pairs={{0,2},{1,3},{2,4},{3,5},{4,6},{5,7},{6,8},{7,9},{8,10},{9,11},{10,... | collective-permute-start | bytes 1204232 | tf_op jit(solution)/shard_map/ppermute | solution.py:295
  16.5 17.5 %collective-permute-start = (bf16[784,256]{1,0:T(8,128)(2,1)}, bf16[784,256]{1,0:T(8,128)(2,1)}, u32[]{:S(2)}, u32[]{:S(2)}) collective-permute-start(bf16[784,256]{1,0:T(8,128)(2,1)} %get-tuple-element.8.refs_3_), channel_id=1, source_target_pairs={{0,254},{1,255},{2,0},{3,1},{4,2},{5,3},{6,4},{7,5},{8,6},{9,7},{1... | collective-permute-start | bytes 1204232 | tf_op jit(solution)/shard_map/ppermute | solution.py:295
  34.0 15.8 %collective-permute-start.1 = (bf16[784,256]{1,0:T(8,128)(2,1)}, bf16[784,256]{1,0:T(8,128)(2,1)}, u32[]{:S(2)}, u32[]{:S(2)}) collective-permute-start(bf16[784,256]{1,0:T(8,128)(2,1)} %collective-permute-done.refs_4_), channel_id=1, source_target_pairs={{0,254},{1,255},{2,0},{3,1},{4,2},{5,3},{6,4},{7,5},{8,6},{9,7},{1... | collective-permute-start | bytes 1204232 | tf_op jit(solution)/shard_map/ppermute | solution.py:295
  41.7 15.5 %collective-permute-start.3 = (bf16[784,256]{1,0:T(8,128)(2,1)}, bf16[784,256]{1,0:T(8,128)(2,1)}, u32[]{:S(2)}, u32[]{:S(2)}) collective-permute-start(bf16[784,256]{1,0:T(8,128)(2,1)} %collective-permute-done.2.refs_3_), channel_id=1, source_target_pairs={{0,2},{1,3},{2,4},{3,5},{4,6},{5,7},{6,8},{7,9},{8,10},{9,11},{10,... | collective-permute-start | bytes 1204232 | tf_op jit(solution)/shard_map/ppermute | solution.py:295
  42.9 21.7 %collective-permute-start.5 = (bf16[784,256]{1,0:T(8,128)(2,1)}, bf16[784,256]{1,0:T(8,128)(2,1)S(1)}, u32[]{:S(2)}, u32[]{:S(2)}) collective-permute-start(bf16[784,256]{1,0:T(8,128)(2,1)} %collective-permute-done.2.refs_3_), channel_id=1, source_target_pairs={{0,1},{1,0},{2,3},{3,2},{4,5},{5,4},{6,7},{7,6},{8,9},{9,8},{10,11... | collective-permute-start | bytes 1204232 | tf_op jit(solution)/shard_map/ppermute | solution.py:298
  44.1 20.6 %collective-permute-start.6 = (bf16[784,256]{1,0:T(8,128)(2,1)}, bf16[784,256]{1,0:T(8,128)(2,1)S(1)}, u32[]{:S(2)}, u32[]{:S(2)}) collective-permute-start(bf16[784,256]{1,0:T(8,128)(2,1)} %collective-permute-done.refs_4_), channel_id=1, source_target_pairs={{0,1},{1,0},{2,3},{3,2},{4,5},{5,4},{6,7},{7,6},{8,9},{9,8},{10,11... | collective-permute-start | bytes 1204232 | tf_op jit(solution)/shard_map/ppermute | solution.py:298
  58.2 16.7 %collective-permute-start.4 = (bf16[784,256]{1,0:T(8,128)(2,1)S(1)}, bf16[784,256]{1,0:T(8,128)(2,1)S(1)}, u32[]{:S(2)}, u32[]{:S(2)}) collective-permute-start(bf16[784,256]{1,0:T(8,128)(2,1)S(1)} %broadcast_select_fusion), channel_id=1, source_target_pairs={{0,1},{1,0},{2,3},{3,2},{4,5},{5,4},{6,7},{7,6},{8,9},{9,8},{10,11... | collective-permute-start | bytes 1204232 | tf_op jit(solution)/shard_map/ppermute | solution.py:298

commit v2 on v1

v2 whole, which is shorter than its diff:
```python
import functools

import jax
import jax.numpy as jnp
from jax import lax
from jax.experimental import pallas as pl
from jax.experimental.pallas import tpu as pltpu
from jax.sharding import PartitionSpec as P

WIN = 4
ROWS = 24
WIDTH = 32
SEQS = 256
STEP = 32
PART = 32
FLAT = ROWS * WIDTH
SENT = FLAT + 16

PROJECT_VMEM = 60 << 20
TILES_VMEM = 44 << 20

BF16 = jnp.bfloat16
F32 = jnp.float32
NT = (((1,), (1,)), ((), ()))


def as_column(row, count):
    width = row.shape[1]
    wide = jnp.broadcast_to(row, (count, width))
    at = lax.broadcasted_iota(jnp.int32, (count, width), 1)
    down = lax.broadcasted_iota(jnp.int32, (count, width), 0)
    return jnp.sum(jnp.where(at == down, wide, 0.0), axis=1, keepdims=True)


HBM = pl.BlockSpec(memory_space=pltpu.HBM)
VMEM = pl.BlockSpec(memory_space=pltpu.VMEM)


def start_all(sources, targets, sems):
    copies = [
        pltpu.make_async_copy(source, target, sems.at[n])
        for n, (source, target) in enumerate(zip(sources, targets))
    ]
    for copy in copies:
        copy.start()
    return copies


def project_kernel(
    depth_hbm,
    lines_hbm,
    scale_hbm,
    shift_hbm,
    first_hbm,
    first_bias_hbm,
    other_hbm,
    other_bias_hbm,
    left_ref,
    right_ref,
    depth_ref,
    lines_ref,
    scale_ref,
    shift_ref,
    first_ref,
    first_bias_ref,
    other_ref,
    other_bias_ref,
    low_ref,
    high_ref,
    maps_ref,
    turn_ref,
    right_low_ref,
    right_high_ref,
    lines_sem,
    small_sem,
):
    steps = SEQS // STEP

    def fetch(s):
        at = pl.ds(pl.multiple_of(s * STEP, STEP), STEP)
        return pltpu.make_async_copy(lines_hbm.at[at], lines_ref.at[at], lines_sem.at[s])

    fetch(0).start()
    small = start_all(
        (scale_hbm, shift_hbm, first_hbm, first_bias_hbm, other_hbm, other_bias_hbm, depth_hbm),
        (scale_ref, shift_ref, first_ref, first_bias_ref, other_ref, other_bias_ref, depth_ref),
        small_sem,
    )
    for s in range(1, steps):
        fetch(s).start()
    for copy in small:
        copy.wait()

    maps_ref[:WIDTH, :] = first_ref[...].astype(F32)
    turned = other_ref[...].astype(F32)
    first_bias = as_column(first_bias_ref[...], WIDTH)
    other_bias = jnp.broadcast_to(as_column(other_bias_ref[...], WIDTH), (WIDTH, 128))
    turn_ref[0] = turned[:, :128]
    turn_ref[1] = turned[:, 128:]
    turn_ref[2] = other_bias
    biases = [jnp.broadcast_to(first_bias, (WIDTH, 128))]
    for k in range(4):
        for half in range(2):
            maps_ref[WIDTH + 8 * k : WIDTH + 8 * k + 8, half * 128 : half * 128 + 128] = turn_ref[
                half, pl.ds(k, 8, stride=4), :
            ]
        biases.append(turn_ref[2, pl.ds(k, 8, stride=4), :])
    bias = jnp.concatenate(biases, axis=0)
    bias = jnp.concatenate([bias, bias], axis=1)
    maps = maps_ref[...].astype(BF16)
    scale = scale_ref[...]
    shift = shift_ref[...]

    def normalise(s, carry):
        fetch(s).wait()
        for c in range(STEP // PART):
            at = pl.ds(pl.multiple_of(s * STEP + c * PART, PART), PART)
            x = lines_ref[at].astype(F32).reshape(PART * ROWS, -1)
            centred = x - jnp.mean(x, axis=1, keepdims=True)
            variance = jnp.mean(centred * centred, axis=1, keepdims=True)
            normed = centred * lax.rsqrt(variance + 1e-05) * scale + shift
            at = pl.ds(pl.multiple_of((s * STEP + c * PART) * ROWS, 8), PART * ROWS)
            low_ref[at, :] = normed[:, :128]
            high_ref[at, :] = normed[:, 128:]
        return carry

    lax.fori_loop(0, steps, normalise, 0)

    seq = lax.broadcasted_iota(jnp.int32, (2 * WIDTH, SEQS), 1)
    lane = lax.broadcasted_iota(jnp.int32, (16, SEQS), 1)
    depths = jnp.zeros((16, SEQS), F32)
    for i in range(ROWS):
        depth = depth_ref[i]
        rows = jnp.concatenate(
            [low_ref[pl.ds(i, SEQS, stride=ROWS), :], high_ref[pl.ds(i, SEQS, stride=ROWS), :]],
            axis=1,
        ).astype(BF16)
        both = lax.dot_general(maps, rows, NT, preferred_element_type=F32) + bias
        both = jnp.where(seq < depth, both, 0.0)
        left_ref[i * WIDTH : (i + 1) * WIDTH, :] = both[:WIDTH].astype(BF16)
        right_low_ref[pl.ds(i, WIDTH, stride=ROWS), :] = both[WIDTH:, :128]
        right_high_ref[pl.ds(i, WIDTH, stride=ROWS), :] = both[WIDTH:, 128:]
        depths = jnp.where(lane == i, depth.astype(F32), depths)
    right_ref[:FLAT, :128] = right_low_ref[...].astype(BF16)
    right_ref[:FLAT, 128:] = right_high_ref[...].astype(BF16)
    right_ref[FLAT:, :] = depths.astype(BF16)


def project(lines, depth, scale, shift, first, first_bias, other, other_bias):
    channels = lines.shape[2]
    return pl.pallas_call(
        project_kernel,
        in_specs=[HBM] * 8,
        out_specs=[VMEM] * 2,
        out_shape=[
            jax.ShapeDtypeStruct((FLAT, SEQS), BF16),
            jax.ShapeDtypeStruct((SENT, SEQS), BF16),
        ],
        scratch_shapes=[
            pltpu.SMEM((ROWS,), jnp.int32),
            pltpu.VMEM((SEQS, ROWS, channels), BF16),
            pltpu.VMEM((1, channels), F32),
            pltpu.VMEM((1, channels), F32),
            pltpu.VMEM((WIDTH, channels), BF16),
            pltpu.VMEM((1, WIDTH), F32),
            pltpu.VMEM((WIDTH, channels), BF16),
            pltpu.VMEM((1, WIDTH), F32),
            pltpu.VMEM((SEQS * ROWS, 128), F32),
            pltpu.VMEM((SEQS * ROWS, 128), F32),
            pltpu.VMEM((2 * WIDTH, channels), F32),
            pltpu.VMEM((3, WIDTH, 128), F32),
            pltpu.VMEM((FLAT, 128), F32),
            pltpu.VMEM((FLAT, 128), F32),
            pltpu.SemaphoreType.DMA((SEQS // STEP,)),
            pltpu.SemaphoreType.DMA((7,)),
        ],
        compiler_params=pltpu.CompilerParams(vmem_limit_bytes=PROJECT_VMEM),
        cost_estimate=pl.CostEstimate(
            flops=2 * 6144 * 256 * 64, bytes_accessed=4 << 20, transcendentals=6144
        ),
        name="project",
    )(
        depth,
        lines,
        scale.reshape(1, -1),
        shift.reshape(1, -1),
        first.T,
        first_bias.reshape(1, -1),
        other.T,
        other_bias.reshape(1, -1),
    )


def tiles_kernel(distances, either, fresh, total, *refs):
    count = len(distances)
    me = lax.axis_index("res")
    side = 1 - 2 * (me % 2)
    depth_hbm, left_ref, *rest = refs
    given = count + int(either)
    right_refs, rest = rest[:given], rest[given:]
    final_in, bias_hbm, couple_hbm, *rest = rest
    if fresh:
        out_hbm, final_ref, *rest = rest
        *rest, final_raw, final_wide = rest
    else:
        final_ref = final_in
        _, out_hbm, *rest = rest
    (
        depth_ref,
        bias_ref,
        picked_ref,
        couple_buf,
        out_buf,
        small_sem,
        take_sem,
        give_sem,
    ) = rest
    blocks = [me + by(side) for by in distances]

    def columns(b):
        place = jnp.clip(blocks[b] - me + WIN, 0, 2 * WIN)
        return pl.ds(pl.multiple_of(place * ROWS, 8), ROWS)

    if fresh:
        final_take = pltpu.make_async_copy(final_in, final_raw, small_sem.at[2])
        final_take.start()
    small = start_all((depth_hbm, bias_hbm), (depth_ref, bias_ref), small_sem)
    takes = start_all(
        [couple_hbm.at[:, :, columns(b), :] for b in range(count)],
        [couple_buf.at[b] for b in range(count)],
        take_sem,
    )
    gives = [
        [
            pltpu.make_async_copy(
                out_buf.at[b, v], out_hbm.at[:, v, columns(b), :], give_sem.at[b, v]
            )
            for b in range(count)
        ]
        for v in range(4)
    ]
    if fresh:
        final_take.wait()
        final_wide[...] = final_raw[...].astype(F32)
        for y in range(0, WIDTH, 2):
            final_ref[y * WIDTH : (y + 2) * WIDTH, :] = jnp.concatenate(
                [final_wide[pl.ds(y + o, WIDTH, stride=WIDTH), :] for o in range(2)], axis=0
            ).astype(BF16)
    for copy in small:
        copy.wait()
    if either:
        picked_ref[...] = jnp.where(side > 0, right_refs[-2][...], right_refs[-1][...])
        right_refs = [*right_refs[:-2], picked_ref]

    group = lax.broadcasted_iota(jnp.int32, (count * 144, 128), 1) // WIDTH
    odd = (group & 1) == 1
    upper = (group & 2) == 2
    bias = bias_ref[...]

    def turned(ref, parts, k):
        return jnp.concatenate(
            [
                ref[(4 * p + (g ^ k)) * WIDTH : (4 * p + (g ^ k) + 1) * WIDTH, :]
                for p in range(parts)
                for g in range(4)
            ],
            axis=0,
        )

    parts = []
    for k in range(4):
        outer = lax.dot_general(
            jnp.concatenate([right[k * 192 : (k + 1) * 192, :] for right in right_refs], axis=0),
            turned(left_ref, 6, k),
            NT,
            preferred_element_type=F32,
        )
        parts.append(
            [
                jnp.concatenate(
                    [
                        outer[
                            b * 192 + q * ROWS : b * 192 + (q + 1) * ROWS, h * 128 : (h + 1) * 128
                        ]
                        for b in range(count)
                        for h in range(6)
                    ],
                    axis=0,
                ).astype(BF16)
                for q in range(8)
            ]
        )
    mixed = [[], [], [], []]
    for q in range(8):
        pair = [jnp.where(odd, parts[k ^ 1][q], parts[k][q]) for k in range(4)]
        for v in range(4):
            mixed[v].append(jnp.where(upper, pair[v ^ 2], pair[v]))
    shares = []
    for b in range(count):
        depth_row = right_refs[b][FLAT : FLAT + 16, :128].astype(F32)[:1, :]
        depth_cols = jnp.broadcast_to(as_column(depth_row, ROWS), (ROWS, 128))
        inside = ((blocks[b] >= 0) & (blocks[b] < total)).astype(F32)
        shares.append((depth_cols, inside))
    for v in range(4):
        sums = jnp.dot(
            jnp.concatenate(mixed[v], axis=1),
            turned(final_ref, 8, v),
            preferred_element_type=F32,
        )
        for b in range(count):
            if v == 0:
                takes[b].wait()
            depth_cols, inside = shares[b]
            for h in range(6):
                depth = depth_ref[4 * h + v].astype(F32)
                pairs = jnp.maximum(jnp.minimum(depth_cols, depth), 1.0)
                update = sums[(b * 6 + h) * ROWS : (b * 6 + h + 1) * ROWS] + bias
                out_buf[b, v, h] = couple_buf[b, h, v] + update * (inside / pairs)
            gives[v][b].start()
    for copies in gives:
        for copy in copies:
            copy.wait()


def form_tiles(distances, either, total, depth, left, rights, final, final_bias, couple, out, name):
    count = len(distances)
    fresh = out is None
    args = [depth, left, *rights, final, final_bias, couple]
    specs = [HBM, VMEM] + [VMEM] * len(rights) + [HBM if fresh else VMEM, HBM, HBM]
    alias = {}
    out_specs = [HBM]
    out_shape = [jax.ShapeDtypeStruct(couple.shape, couple.dtype)]
    extra = []
    if fresh:
        out_specs.append(VMEM)
        out_shape.append(jax.ShapeDtypeStruct(final.shape, final.dtype))
        extra = [pltpu.VMEM(final.shape, BF16), pltpu.VMEM(final.shape, F32)]
    else:
        alias = {len(args): 0}
        args.append(out)
        specs.append(HBM)
    return pl.pallas_call(
        functools.partial(tiles_kernel, distances, either, fresh, total),
        in_specs=specs,
        out_specs=out_specs,
        out_shape=out_shape,
        input_output_aliases=alias,
        scratch_shapes=[
            pltpu.SMEM((ROWS,), jnp.int32),
            pltpu.VMEM((1, 128), F32),
            pltpu.VMEM((SENT, SEQS), BF16),
            pltpu.VMEM((count, 6, 4, ROWS, 128), F32),
            pltpu.VMEM((count, 4, 6, ROWS, 128), F32),
            pltpu.SemaphoreType.DMA((3,)),
            pltpu.SemaphoreType.DMA((count,)),
            pltpu.SemaphoreType.DMA((count, 4)),
            *extra,
        ],
        compiler_params=pltpu.CompilerParams(vmem_limit_bytes=TILES_VMEM),
        cost_estimate=pl.CostEstimate(
            flops=count, bytes_accessed=count, transcendentals=0
        ),
        name=name,
    )(*args)


def on_device(
    homolog_features,
    standardize_scale,
    standardize_shift,
    first_map_matrix,
    first_map_intercept,
    other_map_matrix,
    other_map_intercept,
    final_map_matrix,
    final_map_intercept,
    coverage_lengths,
    couple_features,
):
    total = lax.axis_size("res")
    def moved(block, by):
        return lax.ppermute(block, "res", [(i, (i + by) % total) for i in range(total)])

    def swapped(block):
        return lax.ppermute(block, "res", [(i, i ^ 1) for i in range(total)])

    left, own = project(
        homolog_features,
        coverage_lengths,
        standardize_scale,
        standardize_shift,
        first_map_matrix,
        first_map_intercept,
        other_map_matrix,
        other_map_intercept,
    )
    final_bias = final_map_intercept.reshape(1, -1)

    def tiles(distances, rights, final, out, name, either=False):
        return form_tiles(
            distances,
            either,
            total,
            coverage_lengths,
            left,
            rights,
            final,
            final_bias,
            couple,
            out,
            name,
        )

    couple = couple_features.reshape(ROWS // 4, 4, *couple_features.shape[1:])
    below = moved(own, 2)
    above = moved(own, -2)
    sibling = swapped(own)
    out, final = tiles(
        [lambda side: 0, lambda side: side],
        [own, sibling],
        final_map_matrix,
        None,
        "near",
    )
    below, above, out = lax.optimization_barrier((below, above, out))
    below_far = moved(below, 2)
    above_far = moved(above, -2)
    below_odd = swapped(below)
    above_odd = swapped(above)
    (out,) = tiles(
        [
            lambda side: -2,
            lambda side: 2,
            lambda side: side - 2,
            lambda side: side + 2,
        ],
        [below, above, below_odd, above_odd],
        final,
        out,
        "middle",
    )
    below_far, above_far, out = lax.optimization_barrier((below_far, above_far, out))
    below_far_odd = swapped(below_far)
    above_far_odd = swapped(above_far)
    (out,) = tiles(
        [
            lambda side: -4,
            lambda side: 4,
            lambda side: -3 * side,
        ],
        [below_far, above_far, below_far_odd, above_far_odd],
        final,
        out,
        "far",
        either=True,
    )
    return out.reshape(couple_features.shape)


def solution(mesh):
    return jax.shard_map(
        on_device,
        mesh=mesh,
        in_specs=(
            P(None, "res", None),
            P(),
            P(),
            P(),
            P(),
            P(),
            P(),
            P(),
            P(),
            P("res"),
            P("res", None, None),
        ),
        out_specs=P("res", None, None),
        check_vma=False,
    )
```

time: 77.9 us -> 51.7 us (0.66)
  waiting for transfers between devices: 21.7 us -> 11.2 us
  local copies, waits for them, and re-layouts: 8.1 us -> 2 us
  Pallas kernels: 23 us -> 17.4 us
  starting transfers between devices: 22.9 us -> 20.7 us
  other arithmetic: 1.59 us -> 0 us
    ppermute x4, waiting for transfers between devices: 21.7 us -> 9.25 us  [moved(): lax.ppermute(block, 'res', [(i, (i + by) % total) for i in range(total)])]
    pallas_call x5 -> x4, Pallas kernels: 23 us -> 17.4 us  [the longest x3 11 us: form_tiles(): pl.pallas_call(functools.partial(tiles_kernel, distances, either, fresh,...]
    unnamed x22 -> x12, local copies, waits for them, and re-layouts: 7.04 us -> 2 us
    ppermute x4 -> x5, waiting for transfers between devices: 0.01 us -> 1.94 us  [swapped(): return lax.ppermute(block, 'res', [(i, i ^ 1) for i in range(total)])]
    ppermute x4 -> x5, starting transfers between devices: 6.74 us -> 5.35 us  [swapped(): return lax.ppermute(block, 'res', [(i, i ^ 1) for i in range(total)])]
    reshape x1 -> x0, local copies, waits for them, and re-layouts: 1.06 us -> none  [on_device(): final_map_matrix.reshape(WIDTH, WIDTH, -1).transpose(1, 0, 2)]
    select_n x1 -> x0, other arithmetic: 1.04 us -> none  [on_device(): last = swapped(jnp.where(core == 0, above4, below4))]
  transfers between devices with their start and end apart: 8 -> 9, of which waited for: 3 -> 4; matrix products, arithmetic and copies ran while one was open for 3% -> 0% of each run, Pallas kernels for 18% -> 14%
where the time goes in v2:
time: 51.7 us; the launch traced here: 51.5 us
  starting transfers between devices  20.7 us (40%)
  Pallas kernels  17.4 us (34%)
  waiting for transfers between devices  11.2 us (22%)
  local copies, waits for them, and re-layouts  2 us (4%)
    ppermute x4, starting transfers between devices, moved(): lax.ppermute(block, 'res', [(i, (i + by) % total) for i in range(total)])  15.4 us
    pallas_call x3, Pallas kernels, form_tiles(): pl.pallas_call(functools.partial(tiles_kernel, distances, either, fresh,...  11 us
    ppermute x4, waiting for transfers between devices, moved(): lax.ppermute(block, 'res', [(i, (i + by) % total) for i in range(total)])  9.25 us
    pallas_call x1, Pallas kernels, project(): pl.pallas_call(project_kernel, in_specs=[HBM] * 8, out_specs=[VMEM] * 2,...  6.35 us
    ppermute x5, starting transfers between devices, swapped(): return lax.ppermute(block, 'res', [(i, i ^ 1) for i in range(total)])  5.35 us
    unnamed x12, local copies, waits for them, and re-layouts  2 us
    ppermute x5, waiting for transfers between devices, swapped(): return lax.ppermute(block, 'res', [(i, i ^ 1) for i in range(total)])  1.94 us
  transfers between devices with their start and end apart: 9, of which 4 were waited for; matrix products, arithmetic and copies ran while one was open for 0% of the time, Pallas kernels for 14%

profile of v2, /device:TPU:1, one launch (start us, length us, event | category | flops | bytes accessed | tf_op | source)
XLA Modules:
  0.0 51.5 jit_solution(10497127882633411038)
XLA Ops:
  0.0 0.0 copy-start.4
  0.0 0.0 copy-start.5
  0.0 0.0 copy-start
  0.0 0.0 copy-start.3
  0.0 6.4 %project.1 = (bf16[768,256]{1,0:T(8,128)(2,1)}, bf16[784,256]{1,0:T(8,128)(2,1)}) custom-call(s32[24]{0:T(128)} %refs_0_.5, bf16[256,24,256]{2,1,0:T(8,128)(2,1)} %lines_hbm.1, f32[1,256]{1,0:T(1,128)} %bitcast.17, f32[1,256]{1,0:T(1,128)} %bitcast.18, bf16[32,256]{1,0:T(8,128)(2,1)} %bitcast.15, f32[1,32]{1,0:T(1,128)} %bitcast.19, ...), custom_call_target="tpu_custom_call" | custom-call | flops 201326592 | bytes 4194304 | tf_op jit(solution)/shard_map/project/pallas_call | solution.py:151
  6.4 3.3 %collective-permute-start.2 = (bf16[784,256]{1,0:T(8,128)(2,1)}, bf16[784,256]{1,0:T(8,128)(2,1)S(1)}, u32[]{:S(2)}, u32[]{:S(2)}) collective-permute-start(bf16[784,256]{1,0:T(8,128)(2,1)} %get-tuple-element.16.refs_2_), channel_id=1, source_target_pairs={{0,1},{1,0},{2,3},{3,2},{4,5},{5,4},{6,7},{7,6},{8,9},{9,8},{10,11... | collective-permute-start | bytes 1204232 | tf_op jit(solution)/shard_map/ppermute | solution.py:385
  9.7 0.0 collective-permute-start
  9.7 8.5 %collective-permute-start.1 = (bf16[784,256]{1,0:T(8,128)(2,1)}, bf16[784,256]{1,0:T(8,128)(2,1)S(1)}, u32[]{:S(2)}, u32[]{:S(2)}) collective-permute-start(bf16[784,256]{1,0:T(8,128)(2,1)} %get-tuple-element.16.refs_2_), channel_id=1, source_target_pairs={{0,254},{1,255},{2,0},{3,1},{4,2},{5,3},{6,4},{7,5},{8,6},{9,7},{1... | collective-permute-start | bytes 1204232 | tf_op jit(solution)/shard_map/ppermute | solution.py:382
  18.2 0.0 collective-permute-done.2.refs_3_
  18.2 0.0 copy-done.4
  18.2 0.0 copy-done.5
  18.2 0.0 copy-done
  18.2 0.0 copy-done.3
  18.2 0.0 copy-start.1
  18.2 1.0 %copy-done.1 = bf16[768,256]{1,0:T(8,128)(2,1)S(1)} copy-done((bf16[768,256]{1,0:T(8,128)(2,1)S(1)}, bf16[768,256]{1,0:T(8,128)(2,1)}, u32[]{:S(2)}) %copy-start.1) | copy-done | bytes 393240
  19.2 0.0 copy-start.2
  19.2 1.0 %copy-done.2 = bf16[784,256]{1,0:T(8,128)(2,1)S(1)} copy-done((bf16[784,256]{1,0:T(8,128)(2,1)S(1)}, bf16[784,256]{1,0:T(8,128)(2,1)}, u32[]{:S(2)}) %copy-start.2) | copy-done | bytes 401432
  20.2 3.0 %near.1 = (f32[6,4,216,128]{3,2,1,0:T(8,128)}, bf16[1024,128]{1,0:T(8,128)(2,1)S(1)}) custom-call(s32[24]{0:T(128)S(1)} %copy-done.4, bf16[768,256]{1,0:T(8,128)(2,1)S(1)} %copy-done.1, bf16[784,256]{1,0:T(8,128)(2,1)S(1)} %copy-done.2, bf16[784,256]{1,0:T(8,128)(2,1)S(1)} %collective-permute-done.2.refs_3_, bf16[1024,128]{1,0:T(8,128)(2,1)S(1)} %copy-done.3, ...), custom_call_target="tpu_custom_call" | custom-call | flops 2 | bytes 2 | tf_op jit(solution)/shard_map/near/pallas_call | solution.py:342
  23.3 4.7 %collective-permute-done.refs_2_ = bf16[784,256]{1,0:T(8,128)(2,1)S(1)} collective-permute-done((bf16[784,256]{1,0:T(8,128)(2,1)}, bf16[784,256]{1,0:T(8,128)(2,1)S(1)}, u32[]{:S(2)}, u32[]{:S(2)}) %collective-permute-start) | collective-permute-done | bytes 401440 | tf_op jit(solution)/shard_map/ppermute | solution.py:382
  28.0 0.0 collective-permute-done.1.refs_3_
  28.0 0.7 %collective-permute-start.5 = (bf16[784,256]{1,0:T(8,128)(2,1)S(1)}, bf16[784,256]{1,0:T(8,128)(2,1)S(1)}, u32[]{:S(2)}, u32[]{:S(2)}) collective-permute-start(bf16[784,256]{1,0:T(8,128)(2,1)S(1)} %collective-permute-done.refs_2_), channel_id=1, source_target_pairs={{0,1},{1,0},{2,3},{3,2},{4,5},{5,4},{6,7},{7,6},{8,9},{9,8},{10,11... | collective-permute-start | bytes 1204232 | tf_op jit(solution)/shard_map/ppermute | solution.py:385
  28.6 0.0 collective-permute-start.6
  28.7 0.0 collective-permute-start.3
  28.7 6.9 %collective-permute-start.4 = (bf16[784,256]{1,0:T(8,128)(2,1)S(1)}, bf16[784,256]{1,0:T(8,128)(2,1)S(1)}, u32[]{:S(2)}, u32[]{:S(2)}) collective-permute-start(bf16[784,256]{1,0:T(8,128)(2,1)S(1)} %collective-permute-done.1.refs_3_), channel_id=1, source_target_pairs={{0,254},{1,255},{2,0},{3,1},{4,2},{5,3},{6,4},{7,5},{8,6},{9,7},{1... | collective-permute-start | bytes 1204232 | tf_op jit(solution)/shard_map/ppermute | solution.py:382
  35.5 0.0 collective-permute-done.5.refs_4_
  35.6 0.0 collective-permute-done.6.refs_5_
  35.6 4.3 %middle.1.refs_9_ = f32[6,4,216,128]{3,2,1,0:T(8,128)} custom-call(s32[24]{0:T(128)S(1)} %copy-done.4, bf16[768,256]{1,0:T(8,128)(2,1)S(1)} %copy-done.1, bf16[784,256]{1,0:T(8,128)(2,1)S(1)} %collective-permute-done.refs_2_, bf16[784,256]{1,0:T(8,128)(2,1)S(1)} %collective-permute-done.1.refs_3_, ...), custom_call_target="tpu_custom_call", output_to_operand_aliasing={{}: (9, {})} | custom-call | flops 4 | bytes 4 | tf_op jit(solution)/shard_map/middle/pallas_call | solution.py:342
  39.9 4.5 %collective-permute-done.3.refs_2_ = bf16[784,256]{1,0:T(8,128)(2,1)S(1)} collective-permute-done((bf16[784,256]{1,0:T(8,128)(2,1)S(1)}, bf16[784,256]{1,0:T(8,128)(2,1)S(1)}, u32[]{:S(2)}, u32[]{:S(2)}) %collective-permute-start.3) | collective-permute-done | bytes 401440 | tf_op jit(solution)/shard_map/ppermute | solution.py:382
  44.4 0.0 collective-permute-done.4.refs_3_
  44.4 1.4 %collective-permute-start.7 = (bf16[784,256]{1,0:T(8,128)(2,1)S(1)}, bf16[784,256]{1,0:T(8,128)(2,1)S(1)}, u32[]{:S(2)}, u32[]{:S(2)}) collective-permute-start(bf16[784,256]{1,0:T(8,128)(2,1)S(1)} %collective-permute-done.3.refs_2_), channel_id=1, source_target_pairs={{0,1},{1,0},{2,3},{3,2},{4,5},{5,4},{6,7},{7,6},{8,9},{9,8},{10,11... | collective-permute-start | bytes 1204232 | tf_op jit(solution)/shard_map/ppermute | solution.py:385
  45.8 0.0 collective-permute-start.8
  45.8 1.4 %collective-permute-done.7.refs_4_ = bf16[784,256]{1,0:T(8,128)(2,1)S(1)} collective-permute-done((bf16[784,256]{1,0:T(8,128)(2,1)S(1)}, bf16[784,256]{1,0:T(8,128)(2,1)S(1)}, u32[]{:S(2)}, u32[]{:S(2)}) %collective-permute-start.7) | collective-permute-done | bytes 401440 | tf_op jit(solution)/shard_map/ppermute | solution.py:385
  47.2 0.6 %collective-permute-done.8.refs_5_ = bf16[784,256]{1,0:T(8,128)(2,1)S(1)} collective-permute-done((bf16[784,256]{1,0:T(8,128)(2,1)S(1)}, bf16[784,256]{1,0:T(8,128)(2,1)S(1)}, u32[]{:S(2)}, u32[]{:S(2)}) %collective-permute-start.8) | collective-permute-done | bytes 401440 | tf_op jit(solution)/shard_map/ppermute | solution.py:385
  47.7 3.7 %far.1 = f32[6,4,216,128]{3,2,1,0:T(8,128)} custom-call(s32[24]{0:T(128)S(1)} %copy-done.4, bf16[768,256]{1,0:T(8,128)(2,1)S(1)} %copy-done.1, bf16[784,256]{1,0:T(8,128)(2,1)S(1)} %collective-permute-done.3.refs_2_, bf16[784,256]{1,0:T(8,128)(2,1)S(1)} %collective-permute-done.4.refs_3_, ...), custom_call_target="tpu_custom_call", output_to_operand_aliasing={{}: (9, {})} | custom-call | flops 3 | bytes 3 | tf_op jit(solution)/shard_map/far/pallas_call | solution.py:342
Async XLA Ops:
  0.0 18.2 %copy-start.4 = (s32[24]{0:T(128)S(1)}, s32[24]{0:T(128)}, u32[]{:S(2)}) copy-start(s32[24]{0:T(128)} %refs_0_.5) | copy-start | bytes 292
  0.0 18.2 %copy-start.5 = (f32[128]{0:T(128)S(1)}, f32[128]{0:T(128)}, u32[]{:S(2)}) copy-start(f32[128]{0:T(128)} %param.19) | copy-start | bytes 1540
  0.0 18.2 %copy-start = (f32[24,216,128]{2,1,0:T(8,128)S(1)}, f32[24,216,128]{2,1,0:T(8,128)}, u32[]{:S(2)}) copy-start(f32[24,216,128]{2,1,0:T(8,128)} %param.21) | copy-start | bytes 7962628
  0.0 18.2 %copy-start.3 = (bf16[1024,128]{1,0:T(8,128)(2,1)S(1)}, bf16[1024,128]{1,0:T(8,128)(2,1)}, u32[]{:S(2)}) copy-start(bf16[1024,128]{1,0:T(8,128)(2,1)} %refs_4_.1) | copy-start | bytes 786436
  6.4 11.8 %collective-permute-start.2 = (bf16[784,256]{1,0:T(8,128)(2,1)}, bf16[784,256]{1,0:T(8,128)(2,1)S(1)}, u32[]{:S(2)}, u32[]{:S(2)}) collective-permute-start(bf16[784,256]{1,0:T(8,128)(2,1)} %get-tuple-element.16.refs_2_), channel_id=1, source_target_pairs={{0,1},{1,0},{2,3},{3,2},{4,5},{5,4},{6,7},{7,6},{8,9},{9,8},{10,11... | collective-permute-start | bytes 1204232 | tf_op jit(solution)/shard_map/ppermute | solution.py:385
  9.7 18.3 %collective-permute-start = (bf16[784,256]{1,0:T(8,128)(2,1)}, bf16[784,256]{1,0:T(8,128)(2,1)S(1)}, u32[]{:S(2)}, u32[]{:S(2)}) collective-permute-start(bf16[784,256]{1,0:T(8,128)(2,1)} %get-tuple-element.16.refs_2_), channel_id=1, source_target_pairs={{0,2},{1,3},{2,4},{3,5},{4,6},{5,7},{6,8},{7,9},{8,10},{9,11},{10,... | collective-permute-start | bytes 1204232 | tf_op jit(solution)/shard_map/ppermute | solution.py:382
  9.7 18.3 %collective-permute-start.1 = (bf16[784,256]{1,0:T(8,128)(2,1)}, bf16[784,256]{1,0:T(8,128)(2,1)S(1)}, u32[]{:S(2)}, u32[]{:S(2)}) collective-permute-start(bf16[784,256]{1,0:T(8,128)(2,1)} %get-tuple-element.16.refs_2_), channel_id=1, source_target_pairs={{0,254},{1,255},{2,0},{3,1},{4,2},{5,3},{6,4},{7,5},{8,6},{9,7},{1... | collective-permute-start | bytes 1204232 | tf_op jit(solution)/shard_map/ppermute | solution.py:382
  18.2 1.0 %copy-start.1 = (bf16[768,256]{1,0:T(8,128)(2,1)S(1)}, bf16[768,256]{1,0:T(8,128)(2,1)}, u32[]{:S(2)}) copy-start(bf16[768,256]{1,0:T(8,128)(2,1)} %get-tuple-element.15.refs_1_) | copy-start | bytes 1179652
  19.2 1.0 %copy-start.2 = (bf16[784,256]{1,0:T(8,128)(2,1)S(1)}, bf16[784,256]{1,0:T(8,128)(2,1)}, u32[]{:S(2)}) copy-start(bf16[784,256]{1,0:T(8,128)(2,1)} %get-tuple-element.16.refs_2_) | copy-start | bytes 1204228
  28.0 7.6 %collective-permute-start.5 = (bf16[784,256]{1,0:T(8,128)(2,1)S(1)}, bf16[784,256]{1,0:T(8,128)(2,1)S(1)}, u32[]{:S(2)}, u32[]{:S(2)}) collective-permute-start(bf16[784,256]{1,0:T(8,128)(2,1)S(1)} %collective-permute-done.refs_2_), channel_id=1, source_target_pairs={{0,1},{1,0},{2,3},{3,2},{4,5},{5,4},{6,7},{7,6},{8,9},{9,8},{10,11... | collective-permute-start | bytes 1204232 | tf_op jit(solution)/shard_map/ppermute | solution.py:385
  28.6 6.9 %collective-permute-start.6 = (bf16[784,256]{1,0:T(8,128)(2,1)S(1)}, bf16[784,256]{1,0:T(8,128)(2,1)S(1)}, u32[]{:S(2)}, u32[]{:S(2)}) collective-permute-start(bf16[784,256]{1,0:T(8,128)(2,1)S(1)} %collective-permute-done.1.refs_3_), channel_id=1, source_target_pairs={{0,1},{1,0},{2,3},{3,2},{4,5},{5,4},{6,7},{7,6},{8,9},{9,8},{10,11... | collective-permute-start | bytes 1204232 | tf_op jit(solution)/shard_map/ppermute | solution.py:385
  28.7 15.8 %collective-permute-start.3 = (bf16[784,256]{1,0:T(8,128)(2,1)S(1)}, bf16[784,256]{1,0:T(8,128)(2,1)S(1)}, u32[]{:S(2)}, u32[]{:S(2)}) collective-permute-start(bf16[784,256]{1,0:T(8,128)(2,1)S(1)} %collective-permute-done.refs_2_), channel_id=1, source_target_pairs={{0,2},{1,3},{2,4},{3,5},{4,6},{5,7},{6,8},{7,9},{8,10},{9,11},{10,... | collective-permute-start | bytes 1204232 | tf_op jit(solution)/shard_map/ppermute | solution.py:382
  28.7 15.8 %collective-permute-start.4 = (bf16[784,256]{1,0:T(8,128)(2,1)S(1)}, bf16[784,256]{1,0:T(8,128)(2,1)S(1)}, u32[]{:S(2)}, u32[]{:S(2)}) collective-permute-start(bf16[784,256]{1,0:T(8,128)(2,1)S(1)} %collective-permute-done.1.refs_3_), channel_id=1, source_target_pairs={{0,254},{1,255},{2,0},{3,1},{4,2},{5,3},{6,4},{7,5},{8,6},{9,7},{1... | collective-permute-start | bytes 1204232 | tf_op jit(solution)/shard_map/ppermute | solution.py:382
  44.4 2.7 %collective-permute-start.7 = (bf16[784,256]{1,0:T(8,128)(2,1)S(1)}, bf16[784,256]{1,0:T(8,128)(2,1)S(1)}, u32[]{:S(2)}, u32[]{:S(2)}) collective-permute-start(bf16[784,256]{1,0:T(8,128)(2,1)S(1)} %collective-permute-done.3.refs_2_), channel_id=1, source_target_pairs={{0,1},{1,0},{2,3},{3,2},{4,5},{5,4},{6,7},{7,6},{8,9},{9,8},{10,11... | collective-permute-start | bytes 1204232 | tf_op jit(solution)/shard_map/ppermute | solution.py:385
  45.8 1.9 %collective-permute-start.8 = (bf16[784,256]{1,0:T(8,128)(2,1)S(1)}, bf16[784,256]{1,0:T(8,128)(2,1)S(1)}, u32[]{:S(2)}, u32[]{:S(2)}) collective-permute-start(bf16[784,256]{1,0:T(8,128)(2,1)S(1)} %collective-permute-done.4.refs_3_), channel_id=1, source_target_pairs={{0,1},{1,0},{2,3},{3,2},{4,5},{5,4},{6,7},{7,6},{8,9},{9,8},{10,11... | collective-permute-start | bytes 1204232 | tf_op jit(solution)/shard_map/ppermute | solution.py:385

commit v3 on v2

--- a/solution.py
+++ b/solution.py
@@ -11,8 +11,8 @@
 ROWS = 24
 WIDTH = 32
 SEQS = 256
-STEP = 32
-PART = 32
+STEP = 64
+PART = 64
 FLAT = ROWS * WIDTH
 SENT = FLAT + 16
 
@@ -246,8 +246,6 @@
             final_ref[y * WIDTH : (y + 2) * WIDTH, :] = jnp.concatenate(
                 [final_wide[pl.ds(y + o, WIDTH, stride=WIDTH), :] for o in range(2)], axis=0
             ).astype(BF16)
-    for copy in small:
-        copy.wait()
     if either:
         picked_ref[...] = jnp.where(side > 0, right_refs[-2][...], right_refs[-1][...])
         right_refs = [*right_refs[:-2], picked_ref]
@@ -255,7 +253,6 @@
     group = lax.broadcasted_iota(jnp.int32, (count * 144, 128), 1) // WIDTH
     odd = (group & 1) == 1
     upper = (group & 2) == 2
-    bias = bias_ref[...]
 
     def turned(ref, parts, k):
         return jnp.concatenate(
@@ -301,6 +298,9 @@
         depth_cols = jnp.broadcast_to(as_column(depth_row, ROWS), (ROWS, 128))
         inside = ((blocks[b] >= 0) & (blocks[b] < total)).astype(F32)
         shares.append((depth_cols, inside))
+    for copy in small:
+        copy.wait()
+    bias = bias_ref[...]
     for v in range(4):
         sums = jnp.dot(
             jnp.concatenate(mixed[v], axis=1),
@@ -442,16 +442,13 @@
     below_far, above_far, out = lax.optimization_barrier((below_far, above_far, out))
     below_far_odd = swapped(below_far)
     above_far_odd = swapped(above_far)
+    (out,) = tiles([lambda side: -4, lambda side: 4], [below_far, above_far], final, out, "far")
     (out,) = tiles(
-        [
-            lambda side: -4,
-            lambda side: 4,
-            lambda side: -3 * side,
-        ],
-        [below_far, above_far, below_far_odd, above_far_odd],
+        [lambda side: -3 * side],
+        [below_far_odd, above_far_odd],
         final,
         out,
-        "far",
+        "last",
         either=True,
     )
     return out.reshape(couple_features.shape)

time: 51.7 us -> 50.5 us (0.977)
  waiting for transfers between devices: 11.2 us -> 9.6 us
    ppermute x5, waiting for transfers between devices: 1.94 us -> 0.01 us  [swapped(): return lax.ppermute(block, 'res', [(i, i ^ 1) for i in range(total)])]
    pallas_call x3 -> x4, Pallas kernels: 11 us -> 11.7 us  [form_tiles(): pl.pallas_call(functools.partial(tiles_kernel, distances, either, fresh,...]
  transfers between devices with their start and end apart: 9 -> 9, of which waited for: 4 -> 2; matrix products, arithmetic and copies ran while one was open for 0% -> 0% of each run, Pallas kernels for 14% -> 19%
where the time goes in v3:
time: 50.5 us; the launch traced here: 50.4 us
  starting transfers between devices  20.7 us (41%)
  Pallas kernels  17.8 us (35%)
  waiting for transfers between devices  9.6 us (19%)
  local copies, waits for them, and re-layouts  2 us (4%)
    ppermute x4, starting transfers between devices, moved(): lax.ppermute(block, 'res', [(i, (i + by) % total) for i in range(total)])  15.4 us
    pallas_call x4, Pallas kernels, form_tiles(): pl.pallas_call(functools.partial(tiles_kernel, distances, either, fresh,...  11.7 us
    ppermute x4, waiting for transfers between devices, moved(): lax.ppermute(block, 'res', [(i, (i + by) % total) for i in range(total)])  9.59 us
    pallas_call x1, Pallas kernels, project(): pl.pallas_call(project_kernel, in_specs=[HBM] * 8, out_specs=[VMEM] * 2,...  6.05 us
    ppermute x5, starting transfers between devices, swapped(): return lax.ppermute(block, 'res', [(i, i ^ 1) for i in range(total)])  5.34 us
    unnamed x12, local copies, waits for them, and re-layouts  2 us
  transfers between devices with their start and end apart: 9, of which 2 were waited for; matrix products, arithmetic and copies ran while one was open for 0% of the time, Pallas kernels for 19%

profile of v3, /device:TPU:1, one launch (start us, length us, event | category | flops | bytes accessed | tf_op | source)
XLA Modules:
  0.0 50.4 jit_solution(1343351627429048713)
XLA Ops:
  0.0 0.0 copy-start.4
  0.0 0.0 copy-start.5
  0.0 0.0 copy-start
  0.0 0.0 copy-start.3
  0.0 6.0 %project.1 = (bf16[768,256]{1,0:T(8,128)(2,1)}, bf16[784,256]{1,0:T(8,128)(2,1)}) custom-call(s32[24]{0:T(128)} %refs_0_.7, bf16[256,24,256]{2,1,0:T(8,128)(2,1)} %lines_hbm.1, f32[1,256]{1,0:T(1,128)} %bitcast.19, f32[1,256]{1,0:T(1,128)} %bitcast.20, bf16[32,256]{1,0:T(8,128)(2,1)} %bitcast.17, f32[1,32]{1,0:T(1,128)} %bitcast.21, ...), custom_call_target="tpu_custom_call" | custom-call | flops 201326592 | bytes 4194304 | tf_op jit(solution)/shard_map/project/pallas_call | solution.py:151
  6.1 3.3 %collective-permute-start.2 = (bf16[784,256]{1,0:T(8,128)(2,1)}, bf16[784,256]{1,0:T(8,128)(2,1)S(1)}, u32[]{:S(2)}, u32[]{:S(2)}) collective-permute-start(bf16[784,256]{1,0:T(8,128)(2,1)} %get-tuple-element.16.refs_2_), channel_id=1, source_target_pairs={{0,1},{1,0},{2,3},{3,2},{4,5},{5,4},{6,7},{7,6},{8,9},{9,8},{10,11... | collective-permute-start | bytes 1204232 | tf_op jit(solution)/shard_map/ppermute | solution.py:385
  9.4 0.0 collective-permute-start
  9.4 8.5 %collective-permute-start.1 = (bf16[784,256]{1,0:T(8,128)(2,1)}, bf16[784,256]{1,0:T(8,128)(2,1)S(1)}, u32[]{:S(2)}, u32[]{:S(2)}) collective-permute-start(bf16[784,256]{1,0:T(8,128)(2,1)} %get-tuple-element.16.refs_2_), channel_id=1, source_target_pairs={{0,254},{1,255},{2,0},{3,1},{4,2},{5,3},{6,4},{7,5},{8,6},{9,7},{1... | collective-permute-start | bytes 1204232 | tf_op jit(solution)/shard_map/ppermute | solution.py:382
  17.9 0.0 collective-permute-done.2.refs_3_
  17.9 0.0 copy-done.4
  17.9 0.0 copy-done.5
  17.9 0.0 copy-done
  17.9 0.0 copy-done.3
  17.9 0.0 copy-start.1
  17.9 1.0 %copy-done.1 = bf16[768,256]{1,0:T(8,128)(2,1)S(1)} copy-done((bf16[768,256]{1,0:T(8,128)(2,1)S(1)}, bf16[768,256]{1,0:T(8,128)(2,1)}, u32[]{:S(2)}) %copy-start.1) | copy-done | bytes 393240
  18.9 0.0 copy-start.2
  18.9 1.0 %copy-done.2 = bf16[784,256]{1,0:T(8,128)(2,1)S(1)} copy-done((bf16[784,256]{1,0:T(8,128)(2,1)S(1)}, bf16[784,256]{1,0:T(8,128)(2,1)}, u32[]{:S(2)}) %copy-start.2) | copy-done | bytes 401432
  19.9 3.0 %near.1 = (f32[6,4,216,128]{3,2,1,0:T(8,128)}, bf16[1024,128]{1,0:T(8,128)(2,1)S(1)}) custom-call(s32[24]{0:T(128)S(1)} %copy-done.4, bf16[768,256]{1,0:T(8,128)(2,1)S(1)} %copy-done.1, bf16[784,256]{1,0:T(8,128)(2,1)S(1)} %copy-done.2, bf16[784,256]{1,0:T(8,128)(2,1)S(1)} %collective-permute-done.2.refs_3_, bf16[1024,128]{1,0:T(8,128)(2,1)S(1)} %copy-done.3, ...), custom_call_target="tpu_custom_call" | custom-call | flops 2 | bytes 2 | tf_op jit(solution)/shard_map/near/pallas_call | solution.py:342
  22.9 4.8 %collective-permute-done.refs_2_ = bf16[784,256]{1,0:T(8,128)(2,1)S(1)} collective-permute-done((bf16[784,256]{1,0:T(8,128)(2,1)}, bf16[784,256]{1,0:T(8,128)(2,1)S(1)}, u32[]{:S(2)}, u32[]{:S(2)}) %collective-permute-start) | collective-permute-done | bytes 401440 | tf_op jit(solution)/shard_map/ppermute | solution.py:382
  27.7 0.0 collective-permute-done.1.refs_3_
  27.7 0.7 %collective-permute-start.5 = (bf16[784,256]{1,0:T(8,128)(2,1)S(1)}, bf16[784,256]{1,0:T(8,128)(2,1)S(1)}, u32[]{:S(2)}, u32[]{:S(2)}) collective-permute-start(bf16[784,256]{1,0:T(8,128)(2,1)S(1)} %collective-permute-done.refs_2_), channel_id=1, source_target_pairs={{0,1},{1,0},{2,3},{3,2},{4,5},{5,4},{6,7},{7,6},{8,9},{9,8},{10,11... | collective-permute-start | bytes 1204232 | tf_op jit(solution)/shard_map/ppermute | solution.py:385
  28.3 0.0 collective-permute-start.6
  28.3 0.0 collective-permute-start.3
  28.4 6.9 %collective-permute-start.4 = (bf16[784,256]{1,0:T(8,128)(2,1)S(1)}, bf16[784,256]{1,0:T(8,128)(2,1)S(1)}, u32[]{:S(2)}, u32[]{:S(2)}) collective-permute-start(bf16[784,256]{1,0:T(8,128)(2,1)S(1)} %collective-permute-done.1.refs_3_), channel_id=1, source_target_pairs={{0,254},{1,255},{2,0},{3,1},{4,2},{5,3},{6,4},{7,5},{8,6},{9,7},{1... | collective-permute-start | bytes 1204232 | tf_op jit(solution)/shard_map/ppermute | solution.py:382
  35.2 0.0 collective-permute-done.5.refs_4_
  35.2 0.0 collective-permute-done.6.refs_5_
  35.3 4.1 %middle.1.refs_7_ = f32[6,4,216,128]{3,2,1,0:T(8,128)} custom-call(s32[24]{0:T(128)S(1)} %copy-done.4, bf16[768,256]{1,0:T(8,128)(2,1)S(1)} %copy-done.1, bf16[784,256]{1,0:T(8,128)(2,1)S(1)} %collective-permute-done.refs_2_, bf16[784,256]{1,0:T(8,128)(2,1)S(1)} %collective-permute-done.1.refs_3_, ...), custom_call_target="tpu_custom_call", output_to_operand_aliasing={{}: (9, {})} | custom-call | flops 4 | bytes 4 | tf_op jit(solution)/shard_map/middle/pallas_call | solution.py:342
  39.3 4.8 %collective-permute-done.3.refs_2_ = bf16[784,256]{1,0:T(8,128)(2,1)S(1)} collective-permute-done((bf16[784,256]{1,0:T(8,128)(2,1)S(1)}, bf16[784,256]{1,0:T(8,128)(2,1)S(1)}, u32[]{:S(2)}, u32[]{:S(2)}) %collective-permute-start.3) | collective-permute-done | bytes 401440 | tf_op jit(solution)/shard_map/ppermute | solution.py:382
  44.1 0.0 collective-permute-done.4.refs_3_
  44.1 1.4 %collective-permute-start.7 = (bf16[784,256]{1,0:T(8,128)(2,1)S(1)}, bf16[784,256]{1,0:T(8,128)(2,1)S(1)}, u32[]{:S(2)}, u32[]{:S(2)}) collective-permute-start(bf16[784,256]{1,0:T(8,128)(2,1)S(1)} %collective-permute-done.3.refs_2_), channel_id=1, source_target_pairs={{0,1},{1,0},{2,3},{3,2},{4,5},{5,4},{6,7},{7,6},{8,9},{9,8},{10,11... | collective-permute-start | bytes 1204232 | tf_op jit(solution)/shard_map/ppermute | solution.py:385
  45.5 0.0 collective-permute-start.8
  45.5 2.6 %far.1.refs_7_ = f32[6,4,216,128]{3,2,1,0:T(8,128)} custom-call(s32[24]{0:T(128)S(1)} %copy-done.4, bf16[768,256]{1,0:T(8,128)(2,1)S(1)} %copy-done.1, bf16[784,256]{1,0:T(8,128)(2,1)S(1)} %collective-permute-done.3.refs_2_, bf16[784,256]{1,0:T(8,128)(2,1)S(1)} %collective-permute-done.4.refs_3_, ...), custom_call_target="tpu_custom_call", output_to_operand_aliasing={{}: (7, {})} | custom-call | flops 2 | bytes 2 | tf_op jit(solution)/shard_map/far/pallas_call | solution.py:342
  48.1 0.0 collective-permute-done.7.refs_2_
  48.1 0.0 collective-permute-done.8.refs_3_
  48.1 2.1 %last.1 = f32[6,4,216,128]{3,2,1,0:T(8,128)} custom-call(s32[24]{0:T(128)S(1)} %copy-done.4, bf16[768,256]{1,0:T(8,128)(2,1)S(1)} %copy-done.1, bf16[784,256]{1,0:T(8,128)(2,1)S(1)} %collective-permute-done.7.refs_2_, bf16[784,256]{1,0:T(8,128)(2,1)S(1)} %collective-permute-done.8.refs_3_, ...), custom_call_target="tpu_custom_call", output_to_operand_aliasing={{}: (7, {})} | custom-call | flops 1 | bytes 1 | tf_op jit(solution)/shard_map/last/pallas_call | solution.py:342
Async XLA Ops:
  0.0 17.9 %copy-start.4 = (s32[24]{0:T(128)S(1)}, s32[24]{0:T(128)}, u32[]{:S(2)}) copy-start(s32[24]{0:T(128)} %refs_0_.7) | copy-start | bytes 292
  0.0 17.9 %copy-start.5 = (f32[128]{0:T(128)S(1)}, f32[128]{0:T(128)}, u32[]{:S(2)}) copy-start(f32[128]{0:T(128)} %param.19) | copy-start | bytes 1540
  0.0 17.9 %copy-start = (f32[24,216,128]{2,1,0:T(8,128)S(1)}, f32[24,216,128]{2,1,0:T(8,128)}, u32[]{:S(2)}) copy-start(f32[24,216,128]{2,1,0:T(8,128)} %param.21) | copy-start | bytes 7962628
  0.0 17.9 %copy-start.3 = (bf16[1024,128]{1,0:T(8,128)(2,1)S(1)}, bf16[1024,128]{1,0:T(8,128)(2,1)}, u32[]{:S(2)}) copy-start(bf16[1024,128]{1,0:T(8,128)(2,1)} %refs_4_.1) | copy-start | bytes 786436
  6.1 11.8 %collective-permute-start.2 = (bf16[784,256]{1,0:T(8,128)(2,1)}, bf16[784,256]{1,0:T(8,128)(2,1)S(1)}, u32[]{:S(2)}, u32[]{:S(2)}) collective-permute-start(bf16[784,256]{1,0:T(8,128)(2,1)} %get-tuple-element.16.refs_2_), channel_id=1, source_target_pairs={{0,1},{1,0},{2,3},{3,2},{4,5},{5,4},{6,7},{7,6},{8,9},{9,8},{10,11... | collective-permute-start | bytes 1204232 | tf_op jit(solution)/shard_map/ppermute | solution.py:385
  9.4 18.3 %collective-permute-start = (bf16[784,256]{1,0:T(8,128)(2,1)}, bf16[784,256]{1,0:T(8,128)(2,1)S(1)}, u32[]{:S(2)}, u32[]{:S(2)}) collective-permute-start(bf16[784,256]{1,0:T(8,128)(2,1)} %get-tuple-element.16.refs_2_), channel_id=1, source_target_pairs={{0,2},{1,3},{2,4},{3,5},{4,6},{5,7},{6,8},{7,9},{8,10},{9,11},{10,... | collective-permute-start | bytes 1204232 | tf_op jit(solution)/shard_map/ppermute | solution.py:382
  9.4 18.3 %collective-permute-start.1 = (bf16[784,256]{1,0:T(8,128)(2,1)}, bf16[784,256]{1,0:T(8,128)(2,1)S(1)}, u32[]{:S(2)}, u32[]{:S(2)}) collective-permute-start(bf16[784,256]{1,0:T(8,128)(2,1)} %get-tuple-element.16.refs_2_), channel_id=1, source_target_pairs={{0,254},{1,255},{2,0},{3,1},{4,2},{5,3},{6,4},{7,5},{8,6},{9,7},{1... | collective-permute-start | bytes 1204232 | tf_op jit(solution)/shard_map/ppermute | solution.py:382
  17.9 1.0 %copy-start.1 = (bf16[768,256]{1,0:T(8,128)(2,1)S(1)}, bf16[768,256]{1,0:T(8,128)(2,1)}, u32[]{:S(2)}) copy-start(bf16[768,256]{1,0:T(8,128)(2,1)} %get-tuple-element.15.refs_1_) | copy-start | bytes 1179652
  18.9 1.0 %copy-start.2 = (bf16[784,256]{1,0:T(8,128)(2,1)S(1)}, bf16[784,256]{1,0:T(8,128)(2,1)}, u32[]{:S(2)}) copy-start(bf16[784,256]{1,0:T(8,128)(2,1)} %get-tuple-element.16.refs_2_) | copy-start | bytes 1204228
  27.7 7.6 %collective-permute-start.5 = (bf16[784,256]{1,0:T(8,128)(2,1)S(1)}, bf16[784,256]{1,0:T(8,128)(2,1)S(1)}, u32[]{:S(2)}, u32[]{:S(2)}) collective-permute-start(bf16[784,256]{1,0:T(8,128)(2,1)S(1)} %collective-permute-done.refs_2_), channel_id=1, source_target_pairs={{0,1},{1,0},{2,3},{3,2},{4,5},{5,4},{6,7},{7,6},{8,9},{9,8},{10,11... | collective-permute-start | bytes 1204232 | tf_op jit(solution)/shard_map/ppermute | solution.py:385
  28.3 6.9 %collective-permute-start.6 = (bf16[784,256]{1,0:T(8,128)(2,1)S(1)}, bf16[784,256]{1,0:T(8,128)(2,1)S(1)}, u32[]{:S(2)}, u32[]{:S(2)}) collective-permute-start(bf16[784,256]{1,0:T(8,128)(2,1)S(1)} %collective-permute-done.1.refs_3_), channel_id=1, source_target_pairs={{0,1},{1,0},{2,3},{3,2},{4,5},{5,4},{6,7},{7,6},{8,9},{9,8},{10,11... | collective-permute-start | bytes 1204232 | tf_op jit(solution)/shard_map/ppermute | solution.py:385
  28.3 15.8 %collective-permute-start.3 = (bf16[784,256]{1,0:T(8,128)(2,1)S(1)}, bf16[784,256]{1,0:T(8,128)(2,1)S(1)}, u32[]{:S(2)}, u32[]{:S(2)}) collective-permute-start(bf16[784,256]{1,0:T(8,128)(2,1)S(1)} %collective-permute-done.refs_2_), channel_id=1, source_target_pairs={{0,2},{1,3},{2,4},{3,5},{4,6},{5,7},{6,8},{7,9},{8,10},{9,11},{10,... | collective-permute-start | bytes 1204232 | tf_op jit(solution)/shard_map/ppermute | solution.py:382
  28.4 15.8 %collective-permute-start.4 = (bf16[784,256]{1,0:T(8,128)(2,1)S(1)}, bf16[784,256]{1,0:T(8,128)(2,1)S(1)}, u32[]{:S(2)}, u32[]{:S(2)}) collective-permute-start(bf16[784,256]{1,0:T(8,128)(2,1)S(1)} %collective-permute-done.1.refs_3_), channel_id=1, source_target_pairs={{0,254},{1,255},{2,0},{3,1},{4,2},{5,3},{6,4},{7,5},{8,6},{9,7},{1... | collective-permute-start | bytes 1204232 | tf_op jit(solution)/shard_map/ppermute | solution.py:382
  44.1 4.0 %collective-permute-start.7 = (bf16[784,256]{1,0:T(8,128)(2,1)S(1)}, bf16[784,256]{1,0:T(8,128)(2,1)S(1)}, u32[]{:S(2)}, u32[]{:S(2)}) collective-permute-start(bf16[784,256]{1,0:T(8,128)(2,1)S(1)} %collective-permute-done.3.refs_2_), channel_id=1, source_target_pairs={{0,1},{1,0},{2,3},{3,2},{4,5},{5,4},{6,7},{7,6},{8,9},{9,8},{10,11... | collective-permute-start | bytes 1204232 | tf_op jit(solution)/shard_map/ppermute | solution.py:385
  45.5 2.6 %collective-permute-start.8 = (bf16[784,256]{1,0:T(8,128)(2,1)S(1)}, bf16[784,256]{1,0:T(8,128)(2,1)S(1)}, u32[]{:S(2)}, u32[]{:S(2)}) collective-permute-start(bf16[784,256]{1,0:T(8,128)(2,1)S(1)} %collective-permute-done.4.refs_3_), channel_id=1, source_target_pairs={{0,1},{1,0},{2,3},{3,2},{4,5},{5,4},{6,7},{7,6},{8,9},{9,8},{10,11... | collective-permute-start | bytes 1204232 | tf_op jit(solution)/shard_map/ppermute | solution.py:385

commit v4 on v3

--- a/solution.py
+++ b/solution.py
@@ -12,7 +12,7 @@
 WIDTH = 32
 SEQS = 256
 STEP = 64
-PART = 64
+PART = 32
 FLAT = ROWS * WIDTH
 SENT = FLAT + 16
 
@@ -378,8 +378,9 @@
     couple_features,
 ):
     total = lax.axis_size("res")
-    def moved(block, by):
-        return lax.ppermute(block, "res", [(i, (i + by) % total) for i in range(total)])
+    def passed(block):
+        path = [*range(0, total, 2), *range(total - 1, 0, -2)]
+        return lax.ppermute(block, "res", list(zip(path, path[1:] + path[:1])))
 
     def swapped(block):
         return lax.ppermute(block, "res", [(i, i ^ 1) for i in range(total)])
@@ -412,9 +413,9 @@
         )
 
     couple = couple_features.reshape(ROWS // 4, 4, *couple_features.shape[1:])
-    below = moved(own, 2)
-    above = moved(own, -2)
     sibling = swapped(own)
+    own_next = passed(own)
+    sibling_next = passed(sibling)
     out, final = tiles(
         [lambda side: 0, lambda side: side],
         [own, sibling],
@@ -422,35 +423,29 @@
         None,
         "near",
     )
-    below, above, out = lax.optimization_barrier((below, above, out))
-    below_far = moved(below, 2)
-    above_far = moved(above, -2)
-    below_odd = swapped(below)
-    above_odd = swapped(above)
+    own_next, sibling_next, out = lax.optimization_barrier((own_next, sibling_next, out))
+    own_far = passed(own_next)
+    sibling_far = passed(sibling_next)
+    own_across = swapped(own_next)
+    sibling_across = swapped(sibling_next)
     (out,) = tiles(
         [
-            lambda side: -2,
-            lambda side: 2,
-            lambda side: side - 2,
-            lambda side: side + 2,
+            lambda side: -2 * side,
+            lambda side: -side,
+            lambda side: 3 * side,
+            lambda side: 2 * side,
         ],
-        [below, above, below_odd, above_odd],
+        [own_next, sibling_next, own_across, sibling_across],
         final,
         out,
         "middle",
     )
-    below_far, above_far, out = lax.optimization_barrier((below_far, above_far, out))
-    below_far_odd = swapped(below_far)
-    above_far_odd = swapped(above_far)
-    (out,) = tiles([lambda side: -4, lambda side: 4], [below_far, above_far], final, out, "far")
+    own_far, sibling_far, out = lax.optimization_barrier((own_far, sibling_far, out))
+    last = swapped(sibling_far)
     (out,) = tiles(
-        [lambda side: -3 * side],
-        [below_far_odd, above_far_odd],
-        final,
-        out,
-        "last",
-        either=True,
-    )
+        [lambda side: -4 * side, lambda side: -3 * side], [own_far, sibling_far], final, out, "far"
+    )
+    (out,) = tiles([lambda side: 4 * side], [last], final, out, "last")
     return out.reshape(couple_features.shape)
 
 

time: 50.5 us -> 47.6 us (0.943)
  the two profiles are of different devices: /device:TPU:1 before, /device:TPU:7 now
where the time goes in v4:
time: 47.6 us; the launch traced here: 47.4 us
  starting transfers between devices  19.8 us (42%)
  Pallas kernels  17.6 us (37%)
  waiting for transfers between devices  7.75 us (16%)
  local copies, waits for them, and re-layouts  2 us (4%)
    ppermute x4, starting transfers between devices, passed(): return lax.ppermute(block, 'res', list(zip(path, path[1:] + path[:1])))  15.1 us
    pallas_call x4, Pallas kernels, form_tiles(): pl.pallas_call(functools.partial(tiles_kernel, distances, either, fresh,...  11.7 us
    ppermute x4, waiting for transfers between devices, passed(): return lax.ppermute(block, 'res', list(zip(path, path[1:] + path[:1])))  7.74 us
    pallas_call x1, Pallas kernels, project(): pl.pallas_call(project_kernel, in_specs=[HBM] * 8, out_specs=[VMEM] * 2,...  5.85 us
    ppermute x4, starting transfers between devices, swapped(): return lax.ppermute(block, 'res', [(i, i ^ 1) for i in range(total)])  4.72 us
    unnamed x12, local copies, waits for them, and re-layouts  2 us
  transfers between devices with their start and end apart: 8, of which 3 were waited for; matrix products, arithmetic and copies ran while one was open for 0% of the time, Pallas kernels for 20%

profile of v4, /device:TPU:7, one launch (start us, length us, event | category | flops | bytes accessed | tf_op | source)
XLA Modules:
  0.0 47.4 jit_solution(18000753005478891518)
XLA Ops:
  0.0 0.0 copy-start.4
  0.0 0.0 copy-start.5
  0.0 0.0 copy-start
  0.0 0.0 copy-start.3
  0.0 5.9 %project.1 = (bf16[768,256]{1,0:T(8,128)(2,1)}, bf16[784,256]{1,0:T(8,128)(2,1)}) custom-call(s32[24]{0:T(128)} %refs_0_.7, bf16[256,24,256]{2,1,0:T(8,128)(2,1)} %lines_hbm.1, f32[1,256]{1,0:T(1,128)} %bitcast.19, f32[1,256]{1,0:T(1,128)} %bitcast.20, bf16[32,256]{1,0:T(8,128)(2,1)} %bitcast.17, f32[1,32]{1,0:T(1,128)} %bitcast.21, ...), custom_call_target="tpu_custom_call" | custom-call | flops 201326592 | bytes 4194304 | tf_op jit(solution)/shard_map/project/pallas_call | solution.py:151
  5.9 0.8 %collective-permute-start.1 = (bf16[784,256]{1,0:T(8,128)(2,1)}, bf16[784,256]{1,0:T(8,128)(2,1)S(1)}, u32[]{:S(2)}, u32[]{:S(2)}) collective-permute-start(bf16[784,256]{1,0:T(8,128)(2,1)} %get-tuple-element.16.refs_2_), channel_id=1, source_target_pairs={{0,1},{1,0},{2,3},{3,2},{4,5},{5,4},{6,7},{7,6},{8,9},{9,8},{10,11... | collective-permute-start | bytes 1204232 | tf_op jit(solution)/shard_map/ppermute | solution.py:386
  6.6 8.3 %collective-permute-start = (bf16[784,256]{1,0:T(8,128)(2,1)}, bf16[784,256]{1,0:T(8,128)(2,1)S(1)}, u32[]{:S(2)}, u32[]{:S(2)}) collective-permute-start(bf16[784,256]{1,0:T(8,128)(2,1)} %get-tuple-element.16.refs_2_), channel_id=1, source_target_pairs={{0,2},{2,4},{4,6},{6,8},{8,10},{10,12},{12,14},{14,16},{16,18},{18... | collective-permute-start | bytes 1204232 | tf_op jit(solution)/shard_map/ppermute | solution.py:383
  14.9 0.0 collective-permute-done.1.refs_3_
  14.9 1.6 %collective-permute-start.2 = (bf16[784,256]{1,0:T(8,128)(2,1)S(1)}, bf16[784,256]{1,0:T(8,128)(2,1)S(1)}, u32[]{:S(2)}, u32[]{:S(2)}) collective-permute-start(bf16[784,256]{1,0:T(8,128)(2,1)S(1)} %collective-permute-done.1.refs_3_), channel_id=1, source_target_pairs={{0,2},{2,4},{4,6},{6,8},{8,10},{10,12},{12,14},{14,16},{16,18},{18... | collective-permute-start | bytes 1204232 | tf_op jit(solution)/shard_map/ppermute | solution.py:383
  16.5 0.0 copy-done.4
  16.5 0.0 copy-done.5
  16.5 0.0 copy-done
  16.5 0.0 copy-done.3
  16.5 0.0 copy-start.1
  16.5 1.0 %copy-done.1 = bf16[768,256]{1,0:T(8,128)(2,1)S(1)} copy-done((bf16[768,256]{1,0:T(8,128)(2,1)S(1)}, bf16[768,256]{1,0:T(8,128)(2,1)}, u32[]{:S(2)}) %copy-start.1) | copy-done | bytes 393240
  17.5 0.0 copy-start.2
  17.5 1.0 %copy-done.2 = bf16[784,256]{1,0:T(8,128)(2,1)S(1)} copy-done((bf16[784,256]{1,0:T(8,128)(2,1)S(1)}, bf16[784,256]{1,0:T(8,128)(2,1)}, u32[]{:S(2)}) %copy-start.2) | copy-done | bytes 401432
  18.5 3.0 %near.1 = (f32[6,4,216,128]{3,2,1,0:T(8,128)}, bf16[1024,128]{1,0:T(8,128)(2,1)S(1)}) custom-call(s32[24]{0:T(128)S(1)} %copy-done.4, bf16[768,256]{1,0:T(8,128)(2,1)S(1)} %copy-done.1, bf16[784,256]{1,0:T(8,128)(2,1)S(1)} %copy-done.2, bf16[784,256]{1,0:T(8,128)(2,1)S(1)} %collective-permute-done.1.refs_3_, bf16[1024,128]{1,0:T(8,128)(2,1)S(1)} %copy-done.3, ...), custom_call_target="tpu_custom_call" | custom-call | flops 2 | bytes 2 | tf_op jit(solution)/shard_map/near/pallas_call | solution.py:342
  21.5 0.0 collective-permute-done.refs_2_
  21.5 2.7 %collective-permute-done.2.refs_3_ = bf16[784,256]{1,0:T(8,128)(2,1)S(1)} collective-permute-done((bf16[784,256]{1,0:T(8,128)(2,1)S(1)}, bf16[784,256]{1,0:T(8,128)(2,1)S(1)}, u32[]{:S(2)}, u32[]{:S(2)}) %collective-permute-start.2) | collective-permute-done | bytes 401440 | tf_op jit(solution)/shard_map/ppermute | solution.py:383
  24.3 1.4 %collective-permute-start.5 = (bf16[784,256]{1,0:T(8,128)(2,1)S(1)}, bf16[784,256]{1,0:T(8,128)(2,1)S(1)}, u32[]{:S(2)}, u32[]{:S(2)}) collective-permute-start(bf16[784,256]{1,0:T(8,128)(2,1)S(1)} %collective-permute-done.refs_2_), channel_id=1, source_target_pairs={{0,1},{1,0},{2,3},{3,2},{4,5},{5,4},{6,7},{7,6},{8,9},{9,8},{10,11... | collective-permute-start | bytes 1204232 | tf_op jit(solution)/shard_map/ppermute | solution.py:386
  25.7 0.0 collective-permute-start.6
  25.7 5.2 %collective-permute-start.3 = (bf16[784,256]{1,0:T(8,128)(2,1)S(1)}, bf16[784,256]{1,0:T(8,128)(2,1)S(1)}, u32[]{:S(2)}, u32[]{:S(2)}) collective-permute-start(bf16[784,256]{1,0:T(8,128)(2,1)S(1)} %collective-permute-done.refs_2_), channel_id=1, source_target_pairs={{0,2},{2,4},{4,6},{6,8},{8,10},{10,12},{12,14},{14,16},{16,18},{18... | collective-permute-start | bytes 1204232 | tf_op jit(solution)/shard_map/ppermute | solution.py:383
  30.9 0.0 collective-permute-start.4
  30.9 0.0 collective-permute-done.5.refs_4_
  30.9 0.0 collective-permute-done.6.refs_5_
  30.9 4.1 %middle.1.refs_7_ = f32[6,4,216,128]{3,2,1,0:T(8,128)} custom-call(s32[24]{0:T(128)S(1)} %copy-done.4, bf16[768,256]{1,0:T(8,128)(2,1)S(1)} %copy-done.1, bf16[784,256]{1,0:T(8,128)(2,1)S(1)} %collective-permute-done.refs_2_, bf16[784,256]{1,0:T(8,128)(2,1)S(1)} %collective-permute-done.2.refs_3_, ...), custom_call_target="tpu_custom_call", output_to_operand_aliasing={{}: (9, {})} | custom-call | flops 4 | bytes 4 | tf_op jit(solution)/shard_map/middle/pallas_call | solution.py:342
  35.0 0.7 %collective-permute-done.3.refs_2_ = bf16[784,256]{1,0:T(8,128)(2,1)S(1)} collective-permute-done((bf16[784,256]{1,0:T(8,128)(2,1)S(1)}, bf16[784,256]{1,0:T(8,128)(2,1)S(1)}, u32[]{:S(2)}, u32[]{:S(2)}) %collective-permute-start.3) | collective-permute-done | bytes 401440 | tf_op jit(solution)/shard_map/ppermute | solution.py:383
  35.7 4.3 %collective-permute-done.4.refs_3_ = bf16[784,256]{1,0:T(8,128)(2,1)S(1)} collective-permute-done((bf16[784,256]{1,0:T(8,128)(2,1)S(1)}, bf16[784,256]{1,0:T(8,128)(2,1)S(1)}, u32[]{:S(2)}, u32[]{:S(2)}) %collective-permute-start.4) | collective-permute-done | bytes 401440 | tf_op jit(solution)/shard_map/ppermute | solution.py:383
  40.0 2.6 %collective-permute-start.7 = (bf16[784,256]{1,0:T(8,128)(2,1)S(1)}, bf16[784,256]{1,0:T(8,128)(2,1)S(1)}, u32[]{:S(2)}, u32[]{:S(2)}) collective-permute-start(bf16[784,256]{1,0:T(8,128)(2,1)S(1)} %collective-permute-done.4.refs_3_), channel_id=1, source_target_pairs={{0,1},{1,0},{2,3},{3,2},{4,5},{5,4},{6,7},{7,6},{8,9},{9,8},{10,11... | collective-permute-start | bytes 1204232 | tf_op jit(solution)/shard_map/ppermute | solution.py:386
  42.6 2.6 %far.1.refs_6_ = f32[6,4,216,128]{3,2,1,0:T(8,128)} custom-call(s32[24]{0:T(128)S(1)} %copy-done.4, bf16[768,256]{1,0:T(8,128)(2,1)S(1)} %copy-done.1, bf16[784,256]{1,0:T(8,128)(2,1)S(1)} %collective-permute-done.3.refs_2_, bf16[784,256]{1,0:T(8,128)(2,1)S(1)} %collective-permute-done.4.refs_3_, ...), custom_call_target="tpu_custom_call", output_to_operand_aliasing={{}: (7, {})} | custom-call | flops 2 | bytes 2 | tf_op jit(solution)/shard_map/far/pallas_call | solution.py:342
  45.2 0.0 collective-permute-done.7.refs_2_
  45.2 2.1 %last.1 = f32[6,4,216,128]{3,2,1,0:T(8,128)} custom-call(s32[24]{0:T(128)S(1)} %copy-done.4, bf16[768,256]{1,0:T(8,128)(2,1)S(1)} %copy-done.1, bf16[784,256]{1,0:T(8,128)(2,1)S(1)} %collective-permute-done.7.refs_2_, bf16[1024,128]{1,0:T(8,128)(2,1)S(1)} %get-tuple-element.20.refs_6_.refs_4_.refs_3_, ...), custom_call_target="tpu_custom_call", output_to_operand_aliasing={{}: (6, {})} | custom-call | flops 1 | bytes 1 | tf_op jit(solution)/shard_map/last/pallas_call | solution.py:342
Async XLA Ops:
  0.0 16.5 %copy-start.4 = (s32[24]{0:T(128)S(1)}, s32[24]{0:T(128)}, u32[]{:S(2)}) copy-start(s32[24]{0:T(128)} %refs_0_.7) | copy-start | bytes 292
  0.0 16.5 %copy-start.5 = (f32[128]{0:T(128)S(1)}, f32[128]{0:T(128)}, u32[]{:S(2)}) copy-start(f32[128]{0:T(128)} %param.19) | copy-start | bytes 1540
  0.0 16.5 %copy-start = (f32[24,216,128]{2,1,0:T(8,128)S(1)}, f32[24,216,128]{2,1,0:T(8,128)}, u32[]{:S(2)}) copy-start(f32[24,216,128]{2,1,0:T(8,128)} %param.21) | copy-start | bytes 7962628
  0.0 16.5 %copy-start.3 = (bf16[1024,128]{1,0:T(8,128)(2,1)S(1)}, bf16[1024,128]{1,0:T(8,128)(2,1)}, u32[]{:S(2)}) copy-start(bf16[1024,128]{1,0:T(8,128)(2,1)} %refs_4_.1) | copy-start | bytes 786436
  5.9 9.1 %collective-permute-start.1 = (bf16[784,256]{1,0:T(8,128)(2,1)}, bf16[784,256]{1,0:T(8,128)(2,1)S(1)}, u32[]{:S(2)}, u32[]{:S(2)}) collective-permute-start(bf16[784,256]{1,0:T(8,128)(2,1)} %get-tuple-element.16.refs_2_), channel_id=1, source_target_pairs={{0,1},{1,0},{2,3},{3,2},{4,5},{5,4},{6,7},{7,6},{8,9},{9,8},{10,11... | collective-permute-start | bytes 1204232 | tf_op jit(solution)/shard_map/ppermute | solution.py:386
  6.6 14.9 %collective-permute-start = (bf16[784,256]{1,0:T(8,128)(2,1)}, bf16[784,256]{1,0:T(8,128)(2,1)S(1)}, u32[]{:S(2)}, u32[]{:S(2)}) collective-permute-start(bf16[784,256]{1,0:T(8,128)(2,1)} %get-tuple-element.16.refs_2_), channel_id=1, source_target_pairs={{0,2},{2,4},{4,6},{6,8},{8,10},{10,12},{12,14},{14,16},{16,18},{18... | collective-permute-start | bytes 1204232 | tf_op jit(solution)/shard_map/ppermute | solution.py:383
  14.9 9.3 %collective-permute-start.2 = (bf16[784,256]{1,0:T(8,128)(2,1)S(1)}, bf16[784,256]{1,0:T(8,128)(2,1)S(1)}, u32[]{:S(2)}, u32[]{:S(2)}) collective-permute-start(bf16[784,256]{1,0:T(8,128)(2,1)S(1)} %collective-permute-done.1.refs_3_), channel_id=1, source_target_pairs={{0,2},{2,4},{4,6},{6,8},{8,10},{10,12},{12,14},{14,16},{16,18},{18... | collective-permute-start | bytes 1204232 | tf_op jit(solution)/shard_map/ppermute | solution.py:383
  16.5 1.0 %copy-start.1 = (bf16[768,256]{1,0:T(8,128)(2,1)S(1)}, bf16[768,256]{1,0:T(8,128)(2,1)}, u32[]{:S(2)}) copy-start(bf16[768,256]{1,0:T(8,128)(2,1)} %get-tuple-element.15.refs_1_) | copy-start | bytes 1179652
  17.5 1.0 %copy-start.2 = (bf16[784,256]{1,0:T(8,128)(2,1)S(1)}, bf16[784,256]{1,0:T(8,128)(2,1)}, u32[]{:S(2)}) copy-start(bf16[784,256]{1,0:T(8,128)(2,1)} %get-tuple-element.16.refs_2_) | copy-start | bytes 1204228
  24.3 6.7 %collective-permute-start.5 = (bf16[784,256]{1,0:T(8,128)(2,1)S(1)}, bf16[784,256]{1,0:T(8,128)(2,1)S(1)}, u32[]{:S(2)}, u32[]{:S(2)}) collective-permute-start(bf16[784,256]{1,0:T(8,128)(2,1)S(1)} %collective-permute-done.refs_2_), channel_id=1, source_target_pairs={{0,1},{1,0},{2,3},{3,2},{4,5},{5,4},{6,7},{7,6},{8,9},{9,8},{10,11... | collective-permute-start | bytes 1204232 | tf_op jit(solution)/shard_map/ppermute | solution.py:386
  25.7 5.3 %collective-permute-start.6 = (bf16[784,256]{1,0:T(8,128)(2,1)S(1)}, bf16[784,256]{1,0:T(8,128)(2,1)S(1)}, u32[]{:S(2)}, u32[]{:S(2)}) collective-permute-start(bf16[784,256]{1,0:T(8,128)(2,1)S(1)} %collective-permute-done.2.refs_3_), channel_id=1, source_target_pairs={{0,1},{1,0},{2,3},{3,2},{4,5},{5,4},{6,7},{7,6},{8,9},{9,8},{10,11... | collective-permute-start | bytes 1204232 | tf_op jit(solution)/shard_map/ppermute | solution.py:386
  25.7 10.0 %collective-permute-start.3 = (bf16[784,256]{1,0:T(8,128)(2,1)S(1)}, bf16[784,256]{1,0:T(8,128)(2,1)S(1)}, u32[]{:S(2)}, u32[]{:S(2)}) collective-permute-start(bf16[784,256]{1,0:T(8,128)(2,1)S(1)} %collective-permute-done.refs_2_), channel_id=1, source_target_pairs={{0,2},{2,4},{4,6},{6,8},{8,10},{10,12},{12,14},{14,16},{16,18},{18... | collective-permute-start | bytes 1204232 | tf_op jit(solution)/shard_map/ppermute | solution.py:383
  30.9 9.1 %collective-permute-start.4 = (bf16[784,256]{1,0:T(8,128)(2,1)S(1)}, bf16[784,256]{1,0:T(8,128)(2,1)S(1)}, u32[]{:S(2)}, u32[]{:S(2)}) collective-permute-start(bf16[784,256]{1,0:T(8,128)(2,1)S(1)} %collective-permute-done.2.refs_3_), channel_id=1, source_target_pairs={{0,2},{2,4},{4,6},{6,8},{8,10},{10,12},{12,14},{14,16},{16,18},{18... | collective-permute-start | bytes 1204232 | tf_op jit(solution)/shard_map/ppermute | solution.py:383
  40.0 5.2 %collective-permute-start.7 = (bf16[784,256]{1,0:T(8,128)(2,1)S(1)}, bf16[784,256]{1,0:T(8,128)(2,1)S(1)}, u32[]{:S(2)}, u32[]{:S(2)}) collective-permute-start(bf16[784,256]{1,0:T(8,128)(2,1)S(1)} %collective-permute-done.4.refs_3_), channel_id=1, source_target_pairs={{0,1},{1,0},{2,3},{3,2},{4,5},{5,4},{6,7},{7,6},{8,9},{9,8},{10,11... | collective-permute-start | bytes 1204232 | tf_op jit(solution)/shard_map/ppermute | solution.py:386

commit v5 on v4

--- a/solution.py
+++ b/solution.py
@@ -424,8 +424,8 @@
         "near",
     )
     own_next, sibling_next, out = lax.optimization_barrier((own_next, sibling_next, out))
+    sibling_far = passed(sibling_next)
     own_far = passed(own_next)
-    sibling_far = passed(sibling_next)
     own_across = swapped(own_next)
     sibling_across = swapped(sibling_next)
     (out,) = tiles(
@@ -440,12 +440,15 @@
         out,
         "middle",
     )
-    own_far, sibling_far, out = lax.optimization_barrier((own_far, sibling_far, out))
+    sibling_far, out = lax.optimization_barrier((sibling_far, out))
     last = swapped(sibling_far)
     (out,) = tiles(
-        [lambda side: -4 * side, lambda side: -3 * side], [own_far, sibling_far], final, out, "far"
-    )
-    (out,) = tiles([lambda side: 4 * side], [last], final, out, "last")
+        [lambda side: -4 * side, lambda side: -3 * side, lambda side: 4 * side],
+        [own_far, sibling_far, last],
+        final,
+        out,
+        "far",
+    )
     return out.reshape(couple_features.shape)
 
 

time: 47.6 us -> 45.5 us (0.956)
  the two profiles are of different devices: /device:TPU:7 before, /device:TPU:6 now
where the time goes in v5:
time: 45.5 us; the launch traced here: 45.4 us
  waiting for transfers between devices  22.4 us (49%)
  Pallas kernels  16.2 us (36%)
  starting transfers between devices  4.52 us (10%)
  local copies, waits for them, and re-layouts  2 us (4%)
    ppermute x4, waiting for transfers between devices, passed(): return lax.ppermute(block, 'res', list(zip(path, path[1:] + path[:1])))  20.6 us
    pallas_call x3, Pallas kernels, form_tiles(): pl.pallas_call(functools.partial(tiles_kernel, distances, either, fresh,...  10.4 us
    pallas_call x1, Pallas kernels, project(): pl.pallas_call(project_kernel, in_specs=[HBM] * 8, out_specs=[VMEM] * 2,...  5.85 us
    ppermute x4, starting transfers between devices, passed(): return lax.ppermute(block, 'res', list(zip(path, path[1:] + path[:1])))  3.92 us
    unnamed x12, local copies, waits for them, and re-layouts  2 us
    ppermute x4, waiting for transfers between devices, swapped(): return lax.ppermute(block, 'res', [(i, i ^ 1) for i in range(total)])  1.8 us
  transfers between devices with their start and end apart: 8, of which 6 were waited for; matrix products, arithmetic and copies ran while one was open for 0% of the time, Pallas kernels for 15%

profile of v5, /device:TPU:6, one launch (start us, length us, event | category | flops | bytes accessed | tf_op | source)
XLA Modules:
  0.0 45.4 jit_solution(15429647557085954799)
XLA Ops:
  0.0 0.0 copy-start.4
  0.0 0.0 copy-start.5
  0.0 0.0 copy-start
  0.0 0.0 copy-start.3
  0.0 5.9 %project.1 = (bf16[768,256]{1,0:T(8,128)(2,1)}, bf16[784,256]{1,0:T(8,128)(2,1)}) custom-call(s32[24]{0:T(128)} %refs_0_.5, bf16[256,24,256]{2,1,0:T(8,128)(2,1)} %lines_hbm.1, f32[1,256]{1,0:T(1,128)} %bitcast.17, f32[1,256]{1,0:T(1,128)} %bitcast.18, bf16[32,256]{1,0:T(8,128)(2,1)} %bitcast.15, f32[1,32]{1,0:T(1,128)} %bitcast.19, ...), custom_call_target="tpu_custom_call" | custom-call | flops 201326592 | bytes 4194304 | tf_op jit(solution)/shard_map/project/pallas_call | solution.py:151
  5.9 0.1 collective-permute-start.1
  6.0 2.0 %collective-permute-start = (bf16[784,256]{1,0:T(8,128)(2,1)}, bf16[784,256]{1,0:T(8,128)(2,1)S(1)}, u32[]{:S(2)}, u32[]{:S(2)}) collective-permute-start(bf16[784,256]{1,0:T(8,128)(2,1)} %get-tuple-element.15.refs_2_), channel_id=1, source_target_pairs={{0,2},{2,4},{4,6},{6,8},{8,10},{10,12},{12,14},{14,16},{16,18},{18... | collective-permute-start | bytes 1204232 | tf_op jit(solution)/shard_map/ppermute | solution.py:383
  8.0 0.0 collective-permute-done.1.refs_3_
  8.0 1.9 %collective-permute-start.2 = (bf16[784,256]{1,0:T(8,128)(2,1)S(1)}, bf16[784,256]{1,0:T(8,128)(2,1)S(1)}, u32[]{:S(2)}, u32[]{:S(2)}) collective-permute-start(bf16[784,256]{1,0:T(8,128)(2,1)S(1)} %collective-permute-done.1.refs_3_), channel_id=1, source_target_pairs={{0,2},{2,4},{4,6},{6,8},{8,10},{10,12},{12,14},{14,16},{16,18},{18... | collective-permute-start | bytes 1204232 | tf_op jit(solution)/shard_map/ppermute | solution.py:383
  9.9 0.0 copy-done.4
  9.9 0.0 copy-done.5
  9.9 0.0 copy-done
  9.9 0.0 copy-done.3
  9.9 0.0 copy-start.1
  9.9 1.0 %copy-done.1 = bf16[768,256]{1,0:T(8,128)(2,1)S(1)} copy-done((bf16[768,256]{1,0:T(8,128)(2,1)S(1)}, bf16[768,256]{1,0:T(8,128)(2,1)}, u32[]{:S(2)}) %copy-start.1) | copy-done | bytes 393240
  10.9 0.0 copy-start.2
  10.9 1.0 %copy-done.2 = bf16[784,256]{1,0:T(8,128)(2,1)S(1)} copy-done((bf16[784,256]{1,0:T(8,128)(2,1)S(1)}, bf16[784,256]{1,0:T(8,128)(2,1)}, u32[]{:S(2)}) %copy-start.2) | copy-done | bytes 401432
  11.9 3.0 %near.1 = (f32[6,4,216,128]{3,2,1,0:T(8,128)}, bf16[1024,128]{1,0:T(8,128)(2,1)S(1)}) custom-call(s32[24]{0:T(128)S(1)} %copy-done.4, bf16[768,256]{1,0:T(8,128)(2,1)S(1)} %copy-done.1, bf16[784,256]{1,0:T(8,128)(2,1)S(1)} %copy-done.2, bf16[784,256]{1,0:T(8,128)(2,1)S(1)} %collective-permute-done.1.refs_3_, bf16[1024,128]{1,0:T(8,128)(2,1)S(1)} %copy-done.3, ...), custom_call_target="tpu_custom_call" | custom-call | flops 2 | bytes 2 | tf_op jit(solution)/shard_map/near/pallas_call | solution.py:342
  14.9 5.8 %collective-permute-done.refs_2_ = bf16[784,256]{1,0:T(8,128)(2,1)S(1)} collective-permute-done((bf16[784,256]{1,0:T(8,128)(2,1)}, bf16[784,256]{1,0:T(8,128)(2,1)S(1)}, u32[]{:S(2)}, u32[]{:S(2)}) %collective-permute-start) | collective-permute-done | bytes 401440 | tf_op jit(solution)/shard_map/ppermute | solution.py:383
  20.7 4.3 %collective-permute-done.2.refs_3_ = bf16[784,256]{1,0:T(8,128)(2,1)S(1)} collective-permute-done((bf16[784,256]{1,0:T(8,128)(2,1)S(1)}, bf16[784,256]{1,0:T(8,128)(2,1)S(1)}, u32[]{:S(2)}, u32[]{:S(2)}) %collective-permute-start.2) | collective-permute-done | bytes 401440 | tf_op jit(solution)/shard_map/ppermute | solution.py:383
  25.0 0.0 collective-permute-start.5
  25.0 0.5 %collective-permute-start.6 = (bf16[784,256]{1,0:T(8,128)(2,1)S(1)}, bf16[784,256]{1,0:T(8,128)(2,1)S(1)}, u32[]{:S(2)}, u32[]{:S(2)}) collective-permute-start(bf16[784,256]{1,0:T(8,128)(2,1)S(1)} %collective-permute-done.2.refs_3_), channel_id=1, source_target_pairs={{0,1},{1,0},{2,3},{3,2},{4,5},{5,4},{6,7},{7,6},{8,9},{9,8},{10,11... | collective-permute-start | bytes 1204232 | tf_op jit(solution)/shard_map/ppermute | solution.py:386
  25.5 0.0 collective-permute-start.4
  25.5 0.0 collective-permute-start.3
  25.5 1.2 %collective-permute-done.5.refs_4_ = bf16[784,256]{1,0:T(8,128)(2,1)S(1)} collective-permute-done((bf16[784,256]{1,0:T(8,128)(2,1)S(1)}, bf16[784,256]{1,0:T(8,128)(2,1)S(1)}, u32[]{:S(2)}, u32[]{:S(2)}) %collective-permute-start.5) | collective-permute-done | bytes 401440 | tf_op jit(solution)/shard_map/ppermute | solution.py:386
  26.7 0.6 %collective-permute-done.6.refs_5_ = bf16[784,256]{1,0:T(8,128)(2,1)S(1)} collective-permute-done((bf16[784,256]{1,0:T(8,128)(2,1)S(1)}, bf16[784,256]{1,0:T(8,128)(2,1)S(1)}, u32[]{:S(2)}, u32[]{:S(2)}) %collective-permute-start.6) | collective-permute-done | bytes 401440 | tf_op jit(solution)/shard_map/ppermute | solution.py:386
  27.3 4.1 %middle.1.refs_8_ = f32[6,4,216,128]{3,2,1,0:T(8,128)} custom-call(s32[24]{0:T(128)S(1)} %copy-done.4, bf16[768,256]{1,0:T(8,128)(2,1)S(1)} %copy-done.1, bf16[784,256]{1,0:T(8,128)(2,1)S(1)} %collective-permute-done.refs_2_, bf16[784,256]{1,0:T(8,128)(2,1)S(1)} %collective-permute-done.2.refs_3_, ...), custom_call_target="tpu_custom_call", output_to_operand_aliasing={{}: (9, {})} | custom-call | flops 4 | bytes 4 | tf_op jit(solution)/shard_map/middle/pallas_call | solution.py:342
  31.4 6.2 %collective-permute-done.4.refs_3_ = bf16[784,256]{1,0:T(8,128)(2,1)S(1)} collective-permute-done((bf16[784,256]{1,0:T(8,128)(2,1)S(1)}, bf16[784,256]{1,0:T(8,128)(2,1)S(1)}, u32[]{:S(2)}, u32[]{:S(2)}) %collective-permute-start.4) | collective-permute-done | bytes 401440 | tf_op jit(solution)/shard_map/ppermute | solution.py:383
  37.6 0.0 collective-permute-start.7
  37.6 4.3 %collective-permute-done.3.refs_2_ = bf16[784,256]{1,0:T(8,128)(2,1)S(1)} collective-permute-done((bf16[784,256]{1,0:T(8,128)(2,1)S(1)}, bf16[784,256]{1,0:T(8,128)(2,1)S(1)}, u32[]{:S(2)}, u32[]{:S(2)}) %collective-permute-start.3) | collective-permute-done | bytes 401440 | tf_op jit(solution)/shard_map/ppermute | solution.py:383
  41.9 0.0 collective-permute-done.7.refs_4_
  41.9 3.3 %far.1 = f32[6,4,216,128]{3,2,1,0:T(8,128)} custom-call(s32[24]{0:T(128)S(1)} %copy-done.4, bf16[768,256]{1,0:T(8,128)(2,1)S(1)} %copy-done.1, bf16[784,256]{1,0:T(8,128)(2,1)S(1)} %collective-permute-done.3.refs_2_, bf16[784,256]{1,0:T(8,128)(2,1)S(1)} %collective-permute-done.4.refs_3_, ...), custom_call_target="tpu_custom_call", output_to_operand_aliasing={{}: (8, {})} | custom-call | flops 3 | bytes 3 | tf_op jit(solution)/shard_map/far/pallas_call | solution.py:342
Async XLA Ops:
  0.0 9.9 %copy-start.4 = (s32[24]{0:T(128)S(1)}, s32[24]{0:T(128)}, u32[]{:S(2)}) copy-start(s32[24]{0:T(128)} %refs_0_.5) | copy-start | bytes 292
  0.0 9.9 %copy-start.5 = (f32[128]{0:T(128)S(1)}, f32[128]{0:T(128)}, u32[]{:S(2)}) copy-start(f32[128]{0:T(128)} %param.19) | copy-start | bytes 1540
  0.0 9.9 %copy-start = (f32[24,216,128]{2,1,0:T(8,128)S(1)}, f32[24,216,128]{2,1,0:T(8,128)}, u32[]{:S(2)}) copy-start(f32[24,216,128]{2,1,0:T(8,128)} %param.21) | copy-start | bytes 7962628
  0.0 9.9 %copy-start.3 = (bf16[1024,128]{1,0:T(8,128)(2,1)S(1)}, bf16[1024,128]{1,0:T(8,128)(2,1)}, u32[]{:S(2)}) copy-start(bf16[1024,128]{1,0:T(8,128)(2,1)} %refs_4_.1) | copy-start | bytes 786436
  5.9 2.1 %collective-permute-start.1 = (bf16[784,256]{1,0:T(8,128)(2,1)}, bf16[784,256]{1,0:T(8,128)(2,1)S(1)}, u32[]{:S(2)}, u32[]{:S(2)}) collective-permute-start(bf16[784,256]{1,0:T(8,128)(2,1)} %get-tuple-element.15.refs_2_), channel_id=1, source_target_pairs={{0,1},{1,0},{2,3},{3,2},{4,5},{5,4},{6,7},{7,6},{8,9},{9,8},{10,11... | collective-permute-start | bytes 1204232 | tf_op jit(solution)/shard_map/ppermute | solution.py:386
  6.0 14.7 %collective-permute-start = (bf16[784,256]{1,0:T(8,128)(2,1)}, bf16[784,256]{1,0:T(8,128)(2,1)S(1)}, u32[]{:S(2)}, u32[]{:S(2)}) collective-permute-start(bf16[784,256]{1,0:T(8,128)(2,1)} %get-tuple-element.15.refs_2_), channel_id=1, source_target_pairs={{0,2},{2,4},{4,6},{6,8},{8,10},{10,12},{12,14},{14,16},{16,18},{18... | collective-permute-start | bytes 1204232 | tf_op jit(solution)/shard_map/ppermute | solution.py:383
  8.0 17.0 %collective-permute-start.2 = (bf16[784,256]{1,0:T(8,128)(2,1)S(1)}, bf16[784,256]{1,0:T(8,128)(2,1)S(1)}, u32[]{:S(2)}, u32[]{:S(2)}) collective-permute-start(bf16[784,256]{1,0:T(8,128)(2,1)S(1)} %collective-permute-done.1.refs_3_), channel_id=1, source_target_pairs={{0,2},{2,4},{4,6},{6,8},{8,10},{10,12},{12,14},{14,16},{16,18},{18... | collective-permute-start | bytes 1204232 | tf_op jit(solution)/shard_map/ppermute | solution.py:383
  9.9 1.0 %copy-start.1 = (bf16[768,256]{1,0:T(8,128)(2,1)S(1)}, bf16[768,256]{1,0:T(8,128)(2,1)}, u32[]{:S(2)}) copy-start(bf16[768,256]{1,0:T(8,128)(2,1)} %get-tuple-element.14.refs_1_) | copy-start | bytes 1179652
  10.9 1.0 %copy-start.2 = (bf16[784,256]{1,0:T(8,128)(2,1)S(1)}, bf16[784,256]{1,0:T(8,128)(2,1)}, u32[]{:S(2)}) copy-start(bf16[784,256]{1,0:T(8,128)(2,1)} %get-tuple-element.15.refs_2_) | copy-start | bytes 1204228
  25.0 1.7 %collective-permute-start.5 = (bf16[784,256]{1,0:T(8,128)(2,1)S(1)}, bf16[784,256]{1,0:T(8,128)(2,1)S(1)}, u32[]{:S(2)}, u32[]{:S(2)}) collective-permute-start(bf16[784,256]{1,0:T(8,128)(2,1)S(1)} %collective-permute-done.refs_2_), channel_id=1, source_target_pairs={{0,1},{1,0},{2,3},{3,2},{4,5},{5,4},{6,7},{7,6},{8,9},{9,8},{10,11... | collective-permute-start | bytes 1204232 | tf_op jit(solution)/shard_map/ppermute | solution.py:386
  25.0 2.3 %collective-permute-start.6 = (bf16[784,256]{1,0:T(8,128)(2,1)S(1)}, bf16[784,256]{1,0:T(8,128)(2,1)S(1)}, u32[]{:S(2)}, u32[]{:S(2)}) collective-permute-start(bf16[784,256]{1,0:T(8,128)(2,1)S(1)} %collective-permute-done.2.refs_3_), channel_id=1, source_target_pairs={{0,1},{1,0},{2,3},{3,2},{4,5},{5,4},{6,7},{7,6},{8,9},{9,8},{10,11... | collective-permute-start | bytes 1204232 | tf_op jit(solution)/shard_map/ppermute | solution.py:386
  25.5 12.1 %collective-permute-start.4 = (bf16[784,256]{1,0:T(8,128)(2,1)S(1)}, bf16[784,256]{1,0:T(8,128)(2,1)S(1)}, u32[]{:S(2)}, u32[]{:S(2)}) collective-permute-start(bf16[784,256]{1,0:T(8,128)(2,1)S(1)} %collective-permute-done.2.refs_3_), channel_id=1, source_target_pairs={{0,2},{2,4},{4,6},{6,8},{8,10},{10,12},{12,14},{14,16},{16,18},{18... | collective-permute-start | bytes 1204232 | tf_op jit(solution)/shard_map/ppermute | solution.py:383
  25.5 16.4 %collective-permute-start.3 = (bf16[784,256]{1,0:T(8,128)(2,1)S(1)}, bf16[784,256]{1,0:T(8,128)(2,1)S(1)}, u32[]{:S(2)}, u32[]{:S(2)}) collective-permute-start(bf16[784,256]{1,0:T(8,128)(2,1)S(1)} %collective-permute-done.refs_2_), channel_id=1, source_target_pairs={{0,2},{2,4},{4,6},{6,8},{8,10},{10,12},{12,14},{14,16},{16,18},{18... | collective-permute-start | bytes 1204232 | tf_op jit(solution)/shard_map/ppermute | solution.py:383
  37.6 4.3 %collective-permute-start.7 = (bf16[784,256]{1,0:T(8,128)(2,1)S(1)}, bf16[784,256]{1,0:T(8,128)(2,1)S(1)}, u32[]{:S(2)}, u32[]{:S(2)}) collective-permute-start(bf16[784,256]{1,0:T(8,128)(2,1)S(1)} %collective-permute-done.4.refs_3_), channel_id=1, source_target_pairs={{0,1},{1,0},{2,3},{3,2},{4,5},{5,4},{6,7},{7,6},{8,9},{9,8},{10,11... | collective-permute-start | bytes 1204232 | tf_op jit(solution)/shard_map/ppermute | solution.py:386
